TPU v7x, 32 devices: a whole 2x2x4 slice. The times are simulated.
32 devices in a mesh: ctx: 8 (over y, x, core), ep: 4 (over z).
Axes of the slice: x: 2, y: 2, z: 4, core: 2. Of those that a mesh axis runs over, the one named last changes fastest.
Arguments:
- block_input_rows: bfloat16 [4096, 4096], P(('ctx', 'ep')), may hold values from -6 to 6
- output_gradient: bfloat16 [4096, 4096], P(('ctx', 'ep')), may hold values from -12 to 12
- expert_choice_index: int32 [4096, 8], P(('ctx', 'ep')), may hold values from 0 to 31, all different within a row; in each aligned block of 128 rows (0 to 127, 128 to 255, ...) at most 36 rows name the same one
- routing_weight_rows: float32 [4096, 8], P(('ctx', 'ep')), may hold values from 0.03 to 0.5
- frozen_gate_weight: bfloat16 [32, 4096, 768], P(('ctx', 'ep')), may hold values from -0.09375 to 0.09375
- frozen_up_weight: bfloat16 [32, 4096, 768], P(('ctx', 'ep')), may hold values from -0.09375 to 0.09375
- frozen_down_weight: bfloat16 [32, 768, 4096], P(('ctx', 'ep')), may hold values from -0.21875 to 0.21875
- gate_adapter_inmap: bfloat16 [32, 16, 4096], P(('ctx', 'ep')), may hold values from -0.09375 to 0.09375
- gate_adapter_outmap: bfloat16 [32, 16, 768], P(('ctx', 'ep')), may hold values from -0.21875 to 0.21875
- up_adapter_inmap: bfloat16 [32, 16, 4096], P(('ctx', 'ep')), may hold values from -0.09375 to 0.09375
- up_adapter_outmap: bfloat16 [32, 16, 768], P(('ctx', 'ep')), may hold values from -0.21875 to 0.21875
- down_adapter_inmap: bfloat16 [32, 16, 768], P(('ctx', 'ep')), may hold values from -0.21875 to 0.21875
- down_adapter_outmap: bfloat16 [32, 16, 4096], P(('ctx', 'ep')), may hold values from -0.09375 to 0.09375
- stored_gate_preact: bfloat16 [32, 1152, 768], P(('ctx', 'ep')), may hold values from -8 to 8
- stored_up_preact: bfloat16 [32, 1152, 768], P(('ctx', 'ep')), may hold values from -6 to 6
Outputs:
- grad_in: bfloat16 [4096, 4096], P(('ctx', 'ep'))
- gate_input_gradient: bfloat16 [32, 16, 4096], P(('ctx', 'ep'))
- gate_output_gradient: bfloat16 [32, 16, 768], P(('ctx', 'ep'))
- up_input_gradient: bfloat16 [32, 16, 4096], P(('ctx', 'ep'))
- up_output_gradient: bfloat16 [32, 16, 768], P(('ctx', 'ep'))
- down_input_gradient: bfloat16 [32, 16, 768], P(('ctx', 'ep'))
- down_output_gradient: bfloat16 [32, 16, 4096], P(('ctx', 'ep'))
Inputs may be any that keep to these rules, and one draw needn't show every extreme that they name: `expert_choice_index`: A token names 8 different experts. Among the tokens of one device, an expert is named by at most 36 of them, and in every draw some expert by exactly 36.
All inputs are finite; a program needn't handle non-finite values.
Results may differ from a plain program's by a relative error of at most 0.0065.
Values may be sent and summed in bfloat16 or wider, within the bound.
No kernel may reach another device: no remote copies, remote signals or barrier semaphores. Data moves between devices by JAX's collectives and lax.ppermute only.
A program may use at most 256 MiB of HBM per device.

v0:
```python
import jax
import jax.numpy as jnp
from jax import lax
from jax.sharding import PartitionSpec as P

adapter_scale = 2.0


def contract_matrices(left_mat, right_mat, left_axis, right_axis):
    return lax.dot_general(
        left_mat,
        right_mat,
        (((left_axis,), (right_axis,)), ((), ())),
        preferred_element_type=jnp.float32,
    )


def expert_backward(
    gathered_input_rows,
    gathered_gradient_rows,
    gate_pre,
    up_pre,
    frozen_gate_weight,
    frozen_up_weight,
    frozen_down_weight,
    gate_adapter_input,
    gate_out,
    up_adapter_input,
    up_out,
    down_adapter_input,
    down_adapter_output,
):
    rank_width = gate_adapter_input.shape[0]
    gate_value = gate_pre.astype(jnp.float32)
    up_value = up_pre.astype(jnp.float32)
    sigmoid_gate = jax.nn.sigmoid(gate_value)
    silu_gate = gate_value * sigmoid_gate
    hidden_activation = (silu_gate * up_value).astype(jnp.bfloat16)
    down_adapter_delta = contract_matrices(hidden_activation, down_adapter_input, 1, 1).astype(
        jnp.bfloat16
    )
    adapter_gradient = contract_matrices(gathered_gradient_rows, down_adapter_output, 1, 1).astype(
        jnp.bfloat16
    )
    down_output_gradient = adapter_scale * contract_matrices(
        down_adapter_delta, gathered_gradient_rows, 0, 0
    )
    down_input_gradient = adapter_scale * contract_matrices(
        adapter_gradient, hidden_activation, 0, 0
    )
    hidden_gradient_rows = contract_matrices(
        gathered_gradient_rows, frozen_down_weight, 1, 1
    ) + adapter_scale * contract_matrices(adapter_gradient, down_adapter_input, 1, 0)
    gate_gradient_rows = (
        hidden_gradient_rows * up_value * sigmoid_gate * (1.0 + gate_value * (1.0 - sigmoid_gate))
    ).astype(jnp.bfloat16)
    up_gradient_rows = (hidden_gradient_rows * silu_gate).astype(jnp.bfloat16)
    both_inputs = jnp.concatenate([gate_adapter_input, up_adapter_input], axis=0)
    both_deltas = contract_matrices(gathered_input_rows, both_inputs, 1, 1).astype(jnp.bfloat16)
    gate_adapter_delta = both_deltas[:, :rank_width]
    up_adapter_delta = both_deltas[:, rank_width:]
    gate_output_gradient = adapter_scale * contract_matrices(
        gate_adapter_delta, gate_gradient_rows, 0, 0
    )
    up_output_gradient = adapter_scale * contract_matrices(up_adapter_delta, up_gradient_rows, 0, 0)
    gate_backward_rows = contract_matrices(gate_gradient_rows, gate_out, 1, 1).astype(jnp.bfloat16)
    up_backward_rows = contract_matrices(up_gradient_rows, up_out, 1, 1).astype(jnp.bfloat16)
    both_backward = jnp.concatenate([gate_backward_rows, up_backward_rows], axis=1)
    both_input_gradients = adapter_scale * contract_matrices(
        both_backward, gathered_input_rows, 0, 0
    )
    gate_input_gradient = both_input_gradients[:rank_width]
    up_input_gradient = both_input_gradients[rank_width:]
    left_joined = jnp.concatenate([gate_gradient_rows, up_gradient_rows, both_backward], axis=1)
    scaled_inputs = (both_inputs.astype(jnp.float32) * adapter_scale).astype(jnp.bfloat16)
    right_joined = jnp.concatenate([frozen_gate_weight, frozen_up_weight, scaled_inputs.T], axis=1)
    scattered_output_rows = contract_matrices(left_joined, right_joined, 1, 1)
    expert_outcomes = (
        gate_input_gradient.astype(jnp.bfloat16),
        gate_output_gradient.astype(jnp.bfloat16),
        up_input_gradient.astype(jnp.bfloat16),
        up_output_gradient.astype(jnp.bfloat16),
        down_input_gradient.astype(jnp.bfloat16),
        down_output_gradient.astype(jnp.bfloat16),
    )
    return (scattered_output_rows.astype(jnp.bfloat16), expert_outcomes)


def local(
    block_input_rows,
    output_gradient,
    expert_choice_index,
    routing_weight_rows,
    frozen_gate_weight,
    frozen_up_weight,
    frozen_down_weight,
    gate_adapter_inmap,
    gate_adapter_outmap,
    up_adapter_inmap,
    up_adapter_outmap,
    down_adapter_inmap,
    down_adapter_outmap,
    stored_gate_preact,
    stored_up_preact,
):
    tok_rows, model_width = block_input_rows.shape
    top_count = expert_choice_index.shape[1]
    ctx_count = lax.axis_size("ctx")
    ep_count = lax.axis_size("ep")
    devices = ctx_count * ep_count
    local_exp = frozen_gate_weight.shape[0]
    experts = local_exp * devices
    slot_count = stored_gate_preact.shape[1]
    capacity = slot_count // devices
    pick_count = tok_rows * top_count
    flat_ids = expert_choice_index.reshape(pick_count)
    onehot = (flat_ids[:, None] == jnp.arange(experts, dtype=jnp.int32)[None, :]).astype(
        jnp.bfloat16
    )
    pick_iota = jnp.arange(pick_count, dtype=jnp.int32)
    lower_mask = (pick_iota[:, None] >= pick_iota[None, :]).astype(jnp.bfloat16)
    running = jnp.dot(lower_mask, onehot, preferred_element_type=jnp.float32)
    slot_num = (jnp.sum(onehot.astype(jnp.float32) * running, axis=1) - 1.0).astype(jnp.int32)
    target = flat_ids * capacity + slot_num
    source = jnp.full((experts * capacity,), pick_count, jnp.int32).at[target].set(pick_iota)
    filled = source < pick_count
    pick_safe = jnp.minimum(source, pick_count - 1)
    token_index = jnp.where(filled, pick_safe // top_count, tok_rows)
    weight_flat = routing_weight_rows.reshape(pick_count)
    slot_weight = jnp.where(filled, weight_flat[pick_safe], 0.0)
    zero_row = jnp.zeros((1, model_width), jnp.bfloat16)
    padded_input = jnp.concatenate([block_input_rows, zero_row], axis=0)
    padded_grad = jnp.concatenate([output_gradient, zero_row], axis=0)
    send_rows = padded_input[token_index].reshape(experts, capacity, model_width)
    send_grad = (
        (slot_weight[:, None] * padded_grad[token_index].astype(jnp.float32))
        .astype(jnp.bfloat16)
        .reshape(experts, capacity, model_width)
    )
    got_rows, got_grad = (
        lax.all_to_all(send_rows, ("ctx", "ep"), split_axis=0, concat_axis=1, tiled=True),
        lax.all_to_all(send_grad, ("ctx", "ep"), split_axis=0, concat_axis=1, tiled=True),
    )
    scattered_output_rows, expert_outcomes = jax.vmap(expert_backward)(
        got_rows,
        got_grad,
        stored_gate_preact,
        stored_up_preact,
        frozen_gate_weight,
        frozen_up_weight,
        frozen_down_weight,
        gate_adapter_inmap,
        gate_adapter_outmap,
        up_adapter_inmap,
        up_adapter_outmap,
        down_adapter_inmap,
        down_adapter_outmap,
    )
    returned = lax.all_to_all(
        scattered_output_rows, ("ctx", "ep"), split_axis=1, concat_axis=0, tiled=True
    )
    returned_flat = returned.reshape(experts * capacity, model_width)
    picked = returned_flat[target].reshape(tok_rows, top_count, model_width)
    grad_in = jnp.sum(picked.astype(jnp.float32), axis=1).astype(jnp.bfloat16)
    return (
        grad_in,
        expert_outcomes[0],
        expert_outcomes[1],
        expert_outcomes[2],
        expert_outcomes[3],
        expert_outcomes[4],
        expert_outcomes[5],
    )


def solution(mesh):
    in_specs = (
        P(("ctx", "ep"), None),
        P(("ctx", "ep"), None),
        P(("ctx", "ep"), None),
        P(("ctx", "ep"), None),
        P(("ctx", "ep"), None, None),
        P(("ctx", "ep"), None, None),
        P(("ctx", "ep"), None, None),
        P(("ctx", "ep"), None, None),
        P(("ctx", "ep"), None, None),
        P(("ctx", "ep"), None, None),
        P(("ctx", "ep"), None, None),
        P(("ctx", "ep"), None, None),
        P(("ctx", "ep"), None, None),
        P(("ctx", "ep"), None, None),
        P(("ctx", "ep"), None, None),
    )
    out_specs = (
        P(("ctx", "ep"), None),
        P(("ctx", "ep"), None, None),
        P(("ctx", "ep"), None, None),
        P(("ctx", "ep"), None, None),
        P(("ctx", "ep"), None, None),
        P(("ctx", "ep"), None, None),
        P(("ctx", "ep"), None, None),
    )
    return jax.shard_map(local, mesh=mesh, in_specs=in_specs, out_specs=out_specs, check_vma=False)
```

profile of v0, /device:TPU:0, one launch (start us, length us, event | category | flops | bytes accessed | tf_op | source)
XLA Modules:
  0.0 806.0 jit_solution(9816237633040884613)
XLA Ops:
  8.8 8.1 %gather_fusion.1 = bf16[1152,4096]{1,0:T(8,128)(2,1)} fusion(bf16[129,4096]{1,0:T(8,128)(2,1)S(1)} %concatenate.27, s32[2048]{0:T(1024)S(1)} %get-tuple-element.14), kind=kCustom, calls=%fused_computation.1 | custom fusion | bytes 18878976 | tf_op jit(solution)/shard_map/gather | solution.py:136
  16.8 14.6 %reshape.237 = f32[32,36,4096]{2,1,0:T(8,128)} reshape(bf16[1152,4096]{1,0:T(8,128)(2,1)} %gather_fusion.1) | data formatting | bytes 28311552 | tf_op jit(solution)/shard_map/convert_element_type | solution.py:136
  36.3 12.7 %multiply_convert_fusion = bf16[32,36,4096]{2,1,0:T(8,128)(2,1)} fusion(f32[32,36,4096]{2,1,0:T(8,128)} %reshape.237, f32[32,36]{1,0:T(8,128)S(1)} %mul.98), kind=kLoop, calls=%fused_computation.5 | loop fusion | flops 9437184 | bytes 28316160 | tf_op jit(solution)/shard_map/convert_element_type | solution.py:137
  48.9 7.4 all-to-all-start
  56.5 7.9 gather_fusion.3
  64.4 13.1 %reshape.231 = bf16[32,36,4096]{2,1,0:T(8,128)(2,1)} reshape(bf16[1152,4096]{1,0:T(8,128)(2,1)} %gather_fusion.3) | data formatting | bytes 18874368 | tf_op jit(solution)/shard_map/reshape | solution.py:134
  77.5 205.1 %all-to-all-done = bf16[32,36,4096]{2,1,0:T(8,128)(2,1)} async-done(((bf16[32,36,4096]{2,1,0:T(8,128)(2,1)}), bf16[32,36,4096]{2,1,0:T(8,128)(2,1)}, u32[]{:S(2)}, u32[]{:S(2)}) %all-to-all-start) | async-done | bytes 9437216 | tf_op jit(solution)/shard_map/all_to_all | solution.py:142
  282.5 10.1 %all-to-all-start.2 = ((bf16[32,36,4096]{2,1,0:T(8,128)(2,1)}), bf16[32,36,4096]{2,1,0:T(8,128)(2,1)}, u32[]{:S(2)}, u32[]{:S(2)}) async-start(bf16[32,36,4096]{2,1,0:T(8,128)(2,1)} %reshape.231), calls=%async_computation.2 | async-start | bytes 20971520 | tf_op jit(solution)/shard_map/all_to_all | solution.py:141
  299.4 13.2 %reshape.218 = bf16[1152,4096]{1,0:T(8,128)(2,1)} reshape(bf16[32,36,4096]{2,1,0:T(8,128)(2,1)} %all-to-all-done) | data formatting | bytes 18874368 | tf_op jit(solution)/shard_map/reshape.2
  312.6 6.4 convolution_convert_fusion.5
  319.0 10.9 %fusion.5 = f32[1152,768]{0,1:T(8,128)S(1)} fusion(bf16[1152,4096]{1,0:T(8,128)(2,1)S(1)} %copy-done.3, bf16[1,768,4096]{2,1,0:T(8,128)(2,1)} %param.21), kind=kOutput, calls=%fused_computation.15 | convolution fusion | flops 7247757312 | bytes 19267584 | tf_op jit(solution)/shard_map/vmap()/dot_general | solution.py:10
  334.7 24.2 %fusion.4 = bf16[1,1152,4096]{2,1,0:T(8,128)(2,1)} fusion(bf16[1,4096,32]{2,1,0:T(8,128)(2,1)S(1)} %copy.43, bf16[1,4096,768]{2,1,0:T(8,128)(2,1)} %param.20, bf16[1,4096,768]{2,1,0:T(8,128)(2,1)} %param.19, bf16[1,1152,16]{1,2,0:T(8,128)(2,1)S(1)} %fusion.30, bf16[1,1152,16]{1,2,0:T(8,128)(2,1)S(1)} %fusion.29, bf16[1,1152,768]{1,2,0:T(8,128)(2,1)} %copy-done.4, ...), kind=kOutput, calls=%fused_computation.12 | convolution fusion | flops 14855208960 | bytes 25894912 | tf_op jit(solution)/shard_map/vmap()/dot_general | solution.py:10
  358.9 22.4 %copy.49 = bf16[1,1152,4096]{2,0,1:T(2,128)(2,1)} copy(bf16[1,1152,4096]{2,1,0:T(8,128)(2,1)} %fusion.4) | data formatting | bytes 18874368 | tf_op jit(solution)/shard_map/vmap()/convert_element_type | solution.py:86
  381.8 58.7 %reduce.1 = bf16[1152,4096]{1,0:T(8,128)(2,1)} reduce(bf16[1152,1,4096]{2,1,0:T(2,128)(2,1)} %bitcast.110, bf16[]{:T(256)} %broadcast.135), dimensions={1}, to_apply=%bitcast.107.reduce_sub_computation | reduce | bytes 18874370
  440.5 18.0 %reshape.284 = bf16[32,2,73728]{2,1,0:T(2,128)(2,1)} reshape(bf16[1152,4096]{1,0:T(8,128)(2,1)} %reduce.1) | data formatting | bytes 18874368
  458.5 60.3 %all-to-all-done.2 = bf16[32,36,4096]{2,1,0:T(8,128)(2,1)} async-done(((bf16[32,36,4096]{2,1,0:T(8,128)(2,1)}), bf16[32,36,4096]{2,1,0:T(8,128)(2,1)}, u32[]{:S(2)}, u32[]{:S(2)}) %all-to-all-start.2) | async-done | bytes 9437216 | tf_op jit(solution)/shard_map/all_to_all | solution.py:141
  518.8 9.9 %all-to-all-start.1 = ((bf16[32,2,73728]{2,1,0:T(2,128)(2,1)}), bf16[32,2,73728]{2,1,0:T(2,128)(2,1)}, u32[]{:S(2)}, u32[]{:S(2)}) async-start(bf16[32,2,73728]{2,1,0:T(2,128)(2,1)} %reshape.284), calls=%async_computation.1 | async-start | bytes 18874368 | tf_op jit(solution)/shard_map/all_to_all | solution.py:159
  528.7 13.2 %reshape.232 = bf16[1152,4096]{1,0:T(8,128)(2,1)} reshape(bf16[32,36,4096]{2,1,0:T(8,128)(2,1)} %all-to-all-done.2) | data formatting | bytes 18874368 | tf_op jit(solution)/shard_map/reshape.40
  541.9 6.7 fusion.28
  562.1 170.4 %all-to-all-done.1 = bf16[32,2,73728]{2,1,0:T(2,128)(2,1)} async-done(((bf16[32,2,73728]{2,1,0:T(2,128)(2,1)}), bf16[32,2,73728]{2,1,0:T(2,128)(2,1)}, u32[]{:S(2)}, u32[]{:S(2)}) %all-to-all-start.1) | async-done | bytes 9437216 | tf_op jit(solution)/shard_map/all_to_all | solution.py:159
  732.6 24.4 %reshape.285 = bf16[1152,1,4096]{2,1,0:T(2,128)(2,1)} reshape(bf16[32,2,73728]{2,1,0:T(2,128)(2,1)} %all-to-all-done.1) | data formatting | bytes 18874368
  756.9 18.4 %copy.48 = bf16[1,1152,4096]{2,1,0:T(8,128)(2,1)} copy(bf16[1,1152,4096]{2,0,1:T(2,128)(2,1)} %bitcast.109) | data formatting | bytes 18874368
  775.3 20.3 %gather_fusion.2 = bf16[1024,4096]{1,0:T(8,128)(2,1)} fusion(bf16[1152,4096]{1,0:T(8,128)(2,1)} %bitcast.108, s32[1024]{0:T(1024)S(1)} %broadcast_clamp_fusion), kind=kCustom, calls=%fused_computation.2 | custom fusion | bytes 16781312 | tf_op jit(solution)/shard_map/gather | solution.py:163
  795.6 10.1 %bitcast_reduce_fusion = bf16[128,4096]{1,0:T(8,128)(2,1)} fusion(bf16[1024,4096]{1,0:T(8,128)(2,1)} %gather_fusion.2), kind=kLoop, calls=%fused_computation.14 | loop fusion | flops 3670016 | bytes 9437184 | tf_op jit(solution)/shard_map/reduce_sum | solution.py:164
  (74 shorter events, 38.4 us)
Async XLA Ops:
  0.6 311.9 %copy-start = (bf16[1,16,4096]{2,1,0:T(8,128)(2,1)S(1)}, bf16[1,16,4096]{2,1,0:T(8,128)(2,1)}, u32[]{:S(2)}) copy-start(bf16[1,16,4096]{2,1,0:T(8,128)(2,1)} %param.27) | copy-start | bytes 393220
  3.0 4.3 copy-start.16
  16.8 14.6 %copy-start.18 = (f32[128,8]{0,1:T(8,128)S(1)}, f32[128,8]{0,1:T(8,128)}, u32[]{:S(2)}) copy-start(f32[128,8]{0,1:T(8,128)} %param.18) | copy-start | bytes 12292
  48.9 7.4 copy-start.10
  48.9 233.6 %all-to-all-start = ((bf16[32,36,4096]{2,1,0:T(8,128)(2,1)}), bf16[32,36,4096]{2,1,0:T(8,128)(2,1)}, u32[]{:S(2)}, u32[]{:S(2)}) async-start(bf16[32,36,4096]{2,1,0:T(8,128)(2,1)} %multiply_convert_fusion), calls=%async_computation | async-start | bytes 20971520 | tf_op jit(solution)/shard_map/all_to_all | solution.py:142
  77.5 215.2 %copy-start.11 = (bf16[1,16,4096]{2,1,0:T(8,128)(2,1)S(1)}, bf16[1,16,4096]{2,1,0:T(8,128)(2,1)}, u32[]{:S(2)}) copy-start(bf16[1,16,4096]{2,1,0:T(8,128)(2,1)} %param.22) | copy-start | bytes 393220
  77.5 215.2 %copy-start.12 = (bf16[1,16,4096]{2,1,0:T(8,128)(2,1)S(1)}, bf16[1,16,4096]{2,1,0:T(8,128)(2,1)}, u32[]{:S(2)}) copy-start(bf16[1,16,4096]{2,1,0:T(8,128)(2,1)} %param.24) | copy-start | bytes 393220
  77.5 215.8 %copy-start.7 = (bf16[1,1152,768]{2,1,0:T(8,128)(2,1)S(1)}, bf16[1,1152,768]{2,1,0:T(8,128)(2,1)}, u32[]{:S(2)}) copy-start(bf16[1,1152,768]{2,1,0:T(8,128)(2,1)} %param.29) | copy-start | bytes 5308420
  282.5 236.3 %all-to-all-start.2 = ((bf16[32,36,4096]{2,1,0:T(8,128)(2,1)}), bf16[32,36,4096]{2,1,0:T(8,128)(2,1)}, u32[]{:S(2)}, u32[]{:S(2)}) async-start(bf16[32,36,4096]{2,1,0:T(8,128)(2,1)} %reshape.231), calls=%async_computation.2 | async-start | bytes 20971520 | tf_op jit(solution)/shard_map/all_to_all | solution.py:141
  312.6 6.4 copy-start.3
  318.9 11.0 %copy-start.8 = (bf16[1,1152,768]{1,2,0:T(8,128)(2,1)S(1)}, bf16[1,1152,768]{1,2,0:T(8,128)(2,1)}, u32[]{:S(2)}) copy-start(bf16[1,1152,768]{1,2,0:T(8,128)(2,1)} %copy.41) | copy-start | bytes 5308420
  318.9 11.0 %copy-start.9 = (bf16[1,1152,768]{1,2,0:T(8,128)(2,1)S(1)}, bf16[1,1152,768]{1,2,0:T(8,128)(2,1)}, u32[]{:S(2)}) copy-start(bf16[1,1152,768]{1,2,0:T(8,128)(2,1)} %copy.42) | copy-start | bytes 5308420
  319.0 11.0 %copy-start.15 = (bf16[1,16,768]{2,1,0:T(8,128)(2,1)S(1)}, bf16[1,16,768]{2,1,0:T(8,128)(2,1)}, u32[]{:S(2)}) copy-start(bf16[1,16,768]{2,1,0:T(8,128)(2,1)} %param.26) | copy-start | bytes 73732
  329.9 4.0 copy-start.13
  330.0 4.4 copy-start.14
  332.7 1.3 copy-start.4
  332.7 1.7 copy-start.6
  458.5 70.2 %copy-start.17 = (s32[1024,1]{0,1:T(1,128)S(1)}, s32[1024,1]{0,1:T(1,128)}, u32[]{:S(2)}) copy-start(s32[1024,1]{0,1:T(1,128)} %copy-done.16) | copy-start | bytes 12292
  518.8 213.7 %all-to-all-start.1 = ((bf16[32,2,73728]{2,1,0:T(2,128)(2,1)}), bf16[32,2,73728]{2,1,0:T(2,128)(2,1)}, u32[]{:S(2)}, u32[]{:S(2)}) async-start(bf16[32,2,73728]{2,1,0:T(2,128)(2,1)} %reshape.284), calls=%async_computation.1 | async-start | bytes 18874368 | tf_op jit(solution)/shard_map/all_to_all | solution.py:159
  541.9 9.4 %copy-start.5 = (bf16[1,1152,768]{1,2,0:T(8,128)(2,1)S(1)}, bf16[1,1152,768]{1,2,0:T(8,128)(2,1)}, u32[]{:S(2)}) copy-start(bf16[1,1152,768]{1,2,0:T(8,128)(2,1)} %copy-done.4) | copy-start | bytes 5308420
  541.9 11.8 %copy-start.2 = (bf16[1152,4096]{1,0:T(8,128)(2,1)S(1)}, bf16[1152,4096]{1,0:T(8,128)(2,1)}, u32[]{:S(2)}) copy-start(bf16[1152,4096]{1,0:T(8,128)(2,1)} %reshape.232) | copy-start | bytes 28311556
  775.3 30.4 %copy-start.1 = (bf16[1,16,4096]{2,1,0:T(8,128)(2,1)S(1)}, bf16[1,16,4096]{2,1,0:T(8,128)(2,1)}, u32[]{:S(2)}) copy-start(bf16[1,16,4096]{2,1,0:T(8,128)(2,1)} %param.27) | copy-start | bytes 393220
where the time goes:
time: 818 us; the launch traced here: 806 us
  waiting for transfers between devices  436 us (53%)
  local copies, waits for them, and re-layouts  194 us (24%)
  other arithmetic  82.3 us (10%)
  matrix products  64.8 us (8%)
  starting transfers between devices  27.4 us (3%)
    all_to_all x1, waiting for transfers between devices, local(): lax.all_to_all(send_grad, ('ctx', 'ep'), split_axis=0, concat_axis=1, til...  205 us
    all_to_all x1, waiting for transfers between devices, local(): lax.all_to_all(scattered_output_rows, ('ctx', 'ep'), split_axis=1, concat...  170 us
    unnamed x47, local copies, waits for them, and re-layouts  69.7 us
    dot_general x12, matrix products, contract_matrices(): lax.dot_general(left_mat, right_mat, (((left_axis,), (right_axis,)), ((),...  64.3 us
    all_to_all x1, waiting for transfers between devices, local(): lax.all_to_all(send_rows, ('ctx', 'ep'), split_axis=0, concat_axis=1, til...  60.3 us
    unnamed x1, other arithmetic  58.7 us
    another operation x2, local copies, waits for them, and re-layouts  26.4 us
    convert_element_type x1, local copies, waits for them, and re-layouts, expert_backward(): return (scattered_output_rows.astype(jnp.bfloat16), expert_outcomes)  22.4 us
  transfers between devices with their start and end apart: 3, of which 3 were waited for; matrix products, arithmetic and copies ran while one was open for 27% of the time, Pallas kernels for 0%

commit v1 on v0

v1 whole, which is shorter than its diff:
```python
import jax
import jax.numpy as jnp
from jax import lax
from jax.sharding import PartitionSpec as P

scale = 2.0
chunks = 4


def dot(a, b, da, db):
    return lax.dot_general(
        a, b, (((da,), (db,)), ((), ())), preferred_element_type=jnp.float32
    )


def local(
    x,
    grad,
    ids,
    weights,
    gate_w,
    up_w,
    down_w,
    gate_in,
    gate_out,
    up_in,
    up_out,
    down_in,
    down_out,
    gate_pre,
    up_pre,
):
    gate_w, up_w, down_w = gate_w[0], up_w[0], down_w[0]
    gate_in, gate_out, up_in, up_out = gate_in[0], gate_out[0], up_in[0], up_out[0]
    down_in, down_out, gate_pre, up_pre = down_in[0], down_out[0], gate_pre[0], up_pre[0]
    tok, width = x.shape
    rank = gate_in.shape[0]
    nc, ne = lax.axis_size("ctx"), lax.axis_size("ep")
    slots = gate_pre.shape[0]
    rows = slots // nc
    cap = rows // ne
    me = lax.axis_index("ep")
    cols = width // chunks
    bf, f32 = jnp.bfloat16, jnp.float32

    packed = jnp.concatenate([ids.astype(f32), weights], axis=1)
    packed = lax.all_gather(packed, "ep")
    top = ids.shape[1]
    ids_all = packed[:, :, :top].astype(jnp.int32)
    w_all = packed[:, :, top:]
    mine = jnp.arange(nc, dtype=jnp.int32) * ne + me
    hit = ids_all[:, :, None, :] == mine[None, None, :, None]
    sel = jnp.any(hit, axis=3)
    wt = jnp.sum(jnp.where(hit, w_all[:, :, None, :], 0.0), axis=3)
    iota = jnp.arange(tok, dtype=jnp.int32)
    lower = (iota[:, None] > iota[None, :]).astype(bf)
    place = jnp.einsum("ts,esc->cet", lower, sel.astype(bf), preferred_element_type=f32)
    key = place.astype(jnp.int32) + (jnp.arange(ne, dtype=jnp.int32) * cap)[None, :, None]
    key = jnp.where(jnp.transpose(sel, (2, 0, 1)), key, -1).reshape(nc, 1, ne * tok)
    wt = jnp.transpose(wt, (2, 0, 1)).reshape(nc, 1, ne * tok)
    match = key == jnp.arange(rows, dtype=jnp.int32)[None, :, None]
    pick = match.astype(bf)
    slot_w = jnp.sum(jnp.where(match, wt, 0.0), axis=2, keepdims=True)

    got = []
    for q in range(chunks):
        part = lax.all_gather(grad[:, q * cols : (q + 1) * cols], "ep", tiled=True)
        sent = (dot(pick, part, 2, 0) * slot_w).astype(bf)
        got.append(
            lax.all_to_all(sent, "ctx", split_axis=0, concat_axis=0, tiled=True).reshape(slots, cols)
        )
    both_in = jnp.concatenate([gate_in, up_in], axis=0)
    both_all = lax.all_gather(both_in, "ctx", tiled=True)
    x_all = lax.all_gather(x, "ep", tiled=True)
    lora_tok = dot(x_all, both_all, 1, 1).astype(bf).reshape(ne * tok, nc, 2 * rank)
    lora_slot = jnp.einsum("cjt,tcr->cjr", pick, lora_tok, preferred_element_type=f32).astype(bf)
    lora = lax.all_to_all(lora_slot, "ctx", split_axis=0, concat_axis=0, tiled=True).reshape(
        slots, 2 * rank
    )

    gate_v, up_v = gate_pre.astype(f32), up_pre.astype(f32)
    sig = jax.nn.sigmoid(gate_v)
    silu = gate_v * sig
    hidden = (silu * up_v).astype(bf)
    down_lora = dot(hidden, down_in, 1, 1).astype(bf)
    grad_lora = sum(
        dot(got[q], down_out[:, q * cols : (q + 1) * cols], 1, 1) for q in range(chunks)
    ).astype(bf)
    grad_hidden = sum(
        dot(got[q], down_w[:, q * cols : (q + 1) * cols], 1, 1) for q in range(chunks)
    ) + scale * dot(grad_lora, down_in, 1, 0)
    down_output_gradient = jnp.concatenate(
        [(scale * dot(down_lora, got[q], 0, 0)).astype(bf) for q in range(chunks)], axis=1
    )
    down_input_gradient = (scale * dot(grad_lora, hidden, 0, 0)).astype(bf)
    grad_gate = (grad_hidden * up_v * sig * (1.0 + gate_v * (1.0 - sig))).astype(bf)
    grad_up = (grad_hidden * silu).astype(bf)
    gate_output_gradient = (scale * dot(lora[:, :rank], grad_gate, 0, 0)).astype(bf)
    up_output_gradient = (scale * dot(lora[:, rank:], grad_up, 0, 0)).astype(bf)
    gate_back = dot(grad_gate, gate_out, 1, 1).astype(bf)
    up_back = dot(grad_up, up_out, 1, 1).astype(bf)
    back = jnp.concatenate([gate_back, up_back], axis=1)
    scaled_in = (both_in.astype(f32) * scale).astype(bf)

    back_tok = lax.all_to_all(
        back.reshape(nc, rows, 2 * rank), "ctx", split_axis=0, concat_axis=0, tiled=True
    )
    spread = jnp.einsum("cjr,cjt->crt", back_tok, pick, preferred_element_type=f32).astype(bf)
    share = (scale * dot(spread.reshape(nc * 2 * rank, ne * tok), x_all, 1, 0)).astype(bf)
    share = lax.all_to_all(
        share.reshape(nc, 2 * rank, width), "ctx", split_axis=0, concat_axis=0, tiled=True
    )
    both_input_gradients = jnp.sum(share.astype(f32), axis=0).astype(bf)

    outs = []
    for q in range(chunks):
        at = slice(q * cols, (q + 1) * cols)
        rows_out = (
            dot(grad_gate, gate_w[at], 1, 1)
            + dot(grad_up, up_w[at], 1, 1)
            + dot(back, scaled_in[:, at], 1, 0)
        ).astype(bf)
        returned = lax.all_to_all(
            rows_out.reshape(nc, rows, cols), "ctx", split_axis=0, concat_axis=0, tiled=True
        ).reshape(slots, cols)
        partial = dot(pick.reshape(slots, ne * tok), returned, 0, 0).astype(bf)
        parts = lax.all_to_all(
            partial.reshape(ne, tok, cols), "ep", split_axis=0, concat_axis=0, tiled=True
        )
        outs.append(jnp.sum(parts.astype(f32), axis=0).astype(bf))
    grad_in = jnp.concatenate(outs, axis=1)
    return (
        grad_in,
        both_input_gradients[None, :rank],
        gate_output_gradient[None],
        both_input_gradients[None, rank:],
        up_output_gradient[None],
        down_input_gradient[None],
        down_output_gradient[None],
    )


def solution(mesh):
    flat, deep = P(("ctx", "ep"), None), P(("ctx", "ep"), None, None)
    return jax.shard_map(
        local,
        mesh=mesh,
        in_specs=(flat,) * 4 + (deep,) * 11,
        out_specs=(flat,) + (deep,) * 6,
        check_vma=False,
    )
```

time: 818 us -> 528 us (0.65)
  local copies, waits for them, and re-layouts: 194 us -> 6.14 us
  waiting for transfers between devices: 436 us -> 283 us
  other arithmetic: 82.3 us -> 8.01 us
  matrix products: 64.8 us -> 131 us
  starting transfers between devices: 27.4 us -> 62.3 us
  blocking collectives: 0 us -> 14.9 us
  between operations: 1.22 us -> 15.2 us
    all_to_all x3 -> x15, waiting for transfers between devices: 436 us -> 201 us  [the longest x4 82.4 us: local(): lax.all_to_all(rows_out.reshape(nc, rows, cols), 'ctx', split_axis=0, con...]
    all_gather x0 -> x6, waiting for transfers between devices: none -> 79.5 us  [the longest x4 79.4 us: local(): part = lax.all_gather(grad[:, q * cols:(q + 1) * cols], 'ep', tiled=True)]
    unnamed x47 -> x55, local copies, waits for them, and re-layouts: 69.7 us -> 2.06 us
    dot_general x13 -> x44, matrix products: 64.8 us -> 131 us  [the longest x41 129 us: dot(): lax.dot_general(a, b, (((da,), (db,)), ((), ())), preferred_element_type=...]
    unnamed x1, other arithmetic: 58.7 us -> 0.01 us
    gather x4 -> x0, local copies, waits for them, and re-layouts: 40.8 us -> none  [the longest x1 20.3 us: local(): picked = returned_flat[target].reshape(tok_rows, top_count, model_width)]
    convert_element_type x2 -> x0, local copies, waits for them, and re-layouts: 36.9 us -> none  [the longest x1 22.4 us: expert_backward(): return (scattered_output_rows.astype(jnp.bfloat16), expert_outcomes)]
    all_to_all x3 -> x15, starting transfers between devices: 27.4 us -> 62 us  [the longest x4 17.7 us: local(): lax.all_to_all(rows_out.reshape(nc, rows, cols), 'ctx', split_axis=0, con...]
  transfers between devices with their start and end apart: 3 -> 21, of which waited for: 3 -> 17; matrix products, arithmetic and copies ran while one was open for 27% -> 26% of each run, Pallas kernels for 0% -> 0%
where the time goes in v1:
time: 528 us; the launch traced here: 520 us
  waiting for transfers between devices  283 us (54%)
  matrix products  131 us (25%)
  starting transfers between devices  62.3 us (12%)
  between operations  15.2 us (3%)
  blocking collectives  14.9 us (3%)
  other arithmetic  8.01 us (2%)
  local copies, waits for them, and re-layouts  6.14 us (1%)
    dot_general x41, matrix products, dot(): lax.dot_general(a, b, (((da,), (db,)), ((), ())), preferred_element_type=...  129 us
    all_to_all x4, waiting for transfers between devices, local(): lax.all_to_all(rows_out.reshape(nc, rows, cols), 'ctx', split_axis=0, con...  82.4 us
    all_gather x4, waiting for transfers between devices, local(): part = lax.all_gather(grad[:, q * cols:(q + 1) * cols], 'ep', tiled=True)  79.4 us
    all_to_all x4, waiting for transfers between devices, local(): lax.all_to_all(partial.reshape(ne, tok, cols), 'ep', split_axis=0, concat...  74.6 us
    all_to_all x4, waiting for transfers between devices, local(): lax.all_to_all(sent, 'ctx', split_axis=0, concat_axis=0, tiled=True)  31.1 us
    all_to_all x4, starting transfers between devices, local(): lax.all_to_all(rows_out.reshape(nc, rows, cols), 'ctx', split_axis=0, con...  17.7 us
    all_to_all x4, starting transfers between devices, local(): lax.all_to_all(sent, 'ctx', split_axis=0, concat_axis=0, tiled=True)  17.2 us
    all_to_all x4, starting transfers between devices, local(): lax.all_to_all(partial.reshape(ne, tok, cols), 'ep', split_axis=0, concat...  16.5 us
  transfers between devices with their start and end apart: 21, of which 17 were waited for; matrix products, arithmetic and copies ran while one was open for 26% of the time, Pallas kernels for 0%

profile of v1, /device:TPU:0, one launch (start us, length us, event | category | flops | bytes accessed | tf_op | source)
XLA Modules:
  0.0 519.9 jit_solution(7664176424663789093)
XLA Ops:
  9.5 14.9 %all-gather = f32[512,16]{0,1:T(8,128)S(1)} all-gather(f32[128,16]{0,1:T(8,128)S(1)} %pad_maximum_fusion.3), channel_id=2, replica_groups=mesh['ctx'=8,'ep'=4] {'ep'}, dimensions={0}, use_global_device_ids=true | all-gather | bytes 40960 | tf_op jit(solution)/shard_map/all_gather | solution.py:47
  25.3 15.4 %all-gather.8.cloned.1.call-done = bf16[512,1024]{1,0:T(8,128)(2,1)} async-done(((bf16[128,1024]{1,0:T(8,128)(2,1)}), bf16[512,1024]{1,0:T(8,128)(2,1)}) %all-gather.8.cloned.1.call-update) | async-done | bytes 1048592 | tf_op jit(solution)/shard_map/all_gather | solution.py:67
  50.0 28.6 %all-gather.10.cloned.1.call-done = bf16[512,1024]{1,0:T(8,128)(2,1)} async-done(((bf16[128,1024]{1,0:T(8,128)(2,1)}), bf16[512,1024]{1,0:T(8,128)(2,1)}) %all-gather.10.cloned.1.call-update) | async-done | bytes 1048592 | tf_op jit(solution)/shard_map/all_gather | solution.py:67
  87.5 20.1 %all-gather.12.cloned.1.call-done = bf16[512,1024]{1,0:T(8,128)(2,1)} async-done(((bf16[128,1024]{1,0:T(8,128)(2,1)}), bf16[512,1024]{1,0:T(8,128)(2,1)}) %all-gather.12.cloned.1.call-update) | async-done | bytes 1048592 | tf_op jit(solution)/shard_map/all_gather | solution.py:67
  111.6 4.8 all-to-all-done.1
  121.7 15.4 %all-gather.14.cloned.1.call-done = bf16[512,1024]{1,0:T(8,128)(2,1)} async-done(((bf16[128,1024]{1,0:T(8,128)(2,1)}), bf16[512,1024]{1,0:T(8,128)(2,1)}) %all-gather.14.cloned.1.call-update) | async-done | bytes 1048592 | tf_op jit(solution)/shard_map/all_gather | solution.py:67
  144.2 7.2 %all-to-all-done.2 = bf16[8,144,1024]{2,1,0:T(8,128)(2,1)} async-done(((bf16[8,144,1024]{2,1,0:T(8,128)(2,1)}), bf16[8,144,1024]{2,1,0:T(8,128)(2,1)}, u32[]{:S(2)}, u32[]{:S(2)}) %all-to-all-start.2) | async-done | bytes 2359328 | tf_op jit(solution)/shard_map/all_to_all | solution.py:70
  151.4 4.8 all-to-all-start.3
  166.3 5.5 %convolution_add_fusion.5 = f32[1152,768]{1,0:T(8,128)} fusion(f32[1152,768]{1,0:T(8,128)S(1)} %convolution_add_fusion.6, bf16[1152,1024]{1,0:T(8,128)(2,1)} %bitcast.12, bf16[768,4096]{1,0:T(8,128)(2,1)S(1)} %bitcast.236), kind=kOutput, calls=%fused_computation.23 | convolution fusion | flops 1812824064 | bytes 11010048 | tf_op jit(solution)/shard_map/dot_general | solution.py:11
  171.8 19.1 %all-to-all-done.3 = bf16[8,144,1024]{2,1,0:T(8,128)(2,1)} async-done(((bf16[8,144,1024]{2,1,0:T(8,128)(2,1)}), bf16[8,144,1024]{2,1,0:T(8,128)(2,1)}, u32[]{:S(2)}, u32[]{:S(2)}) %all-to-all-start.3) | async-done | bytes 2359328 | tf_op jit(solution)/shard_map/all_to_all | solution.py:70
  193.3 5.4 %convolution_add_fusion.4 = f32[1152,768]{1,0:T(8,128)S(1)} fusion(f32[1152,768]{1,0:T(8,128)} %convolution_add_fusion.5, bf16[1152,1024]{1,0:T(8,128)(2,1)} %bitcast.14, bf16[768,4096]{1,0:T(8,128)(2,1)} %bitcast.232), kind=kOutput, calls=%fused_computation.22 | convolution fusion | flops 1812824064 | bytes 11010048 | tf_op jit(solution)/shard_map/dot_general | solution.py:11
  232.7 19.1 %all-to-all-done.4 = bf16[8,144,1024]{2,1,0:T(8,128)(2,1)} async-done(((bf16[8,144,1024]{2,1,0:T(8,128)(2,1)}), bf16[8,144,1024]{2,1,0:T(8,128)(2,1)}, u32[]{:S(2)}, u32[]{:S(2)}) %all-to-all-start.4) | async-done | bytes 2359328 | tf_op jit(solution)/shard_map/all_to_all | solution.py:123
  251.8 4.4 all-to-all-start.6
  266.0 19.6 %all-to-all-done.6 = bf16[8,144,1024]{2,1,0:T(8,128)(2,1)} async-done(((bf16[8,144,1024]{2,1,0:T(8,128)(2,1)}), bf16[8,144,1024]{2,1,0:T(8,128)(2,1)}, u32[]{:S(2)}, u32[]{:S(2)}) %all-to-all-start.6) | async-done | bytes 2359328 | tf_op jit(solution)/shard_map/all_to_all | solution.py:123
  285.6 4.6 all-to-all-start.8
  300.1 19.6 %all-to-all-done.8 = bf16[8,144,1024]{2,1,0:T(8,128)(2,1)} async-done(((bf16[8,144,1024]{2,1,0:T(8,128)(2,1)}), bf16[8,144,1024]{2,1,0:T(8,128)(2,1)}, u32[]{:S(2)}, u32[]{:S(2)}) %all-to-all-start.8) | async-done | bytes 2359328 | tf_op jit(solution)/shard_map/all_to_all | solution.py:123
  319.7 4.4 all-to-all-start.10
  329.5 24.1 %all-to-all-done.10 = bf16[8,144,1024]{2,1,0:T(8,128)(2,1)} async-done(((bf16[8,144,1024]{2,1,0:T(8,128)(2,1)}), bf16[8,144,1024]{2,1,0:T(8,128)(2,1)}, u32[]{:S(2)}, u32[]{:S(2)}) %all-to-all-start.10) | async-done | bytes 2359328 | tf_op jit(solution)/shard_map/all_to_all | solution.py:123
  370.8 21.6 %all-to-all-done.5 = bf16[4,128,1024]{2,1,0:T(8,128)(2,1)S(1)} async-done(((bf16[4,128,1024]{2,1,0:T(8,128)(2,1)}), bf16[4,128,1024]{2,1,0:T(8,128)(2,1)S(1)}, u32[]{:S(2)}, u32[]{:S(2)}) %all-to-all-start.5) | async-done | bytes 1048608 | tf_op jit(solution)/shard_map/all_to_all | solution.py:127
  400.8 21.1 %all-to-all-done.7 = bf16[4,128,1024]{2,1,0:T(8,128)(2,1)} async-done(((bf16[4,128,1024]{2,1,0:T(8,128)(2,1)}), bf16[4,128,1024]{2,1,0:T(8,128)(2,1)}, u32[]{:S(2)}, u32[]{:S(2)}) %all-to-all-start.7) | async-done | bytes 1048608 | tf_op jit(solution)/shard_map/all_to_all | solution.py:127
  421.9 4.5 all-to-all-start.9
  433.8 17.9 %all-to-all-done.9 = bf16[4,128,1024]{2,1,0:T(8,128)(2,1)} async-done(((bf16[4,128,1024]{2,1,0:T(8,128)(2,1)}), bf16[4,128,1024]{2,1,0:T(8,128)(2,1)}, u32[]{:S(2)}, u32[]{:S(2)}) %all-to-all-start.9) | async-done | bytes 1048608 | tf_op jit(solution)/shard_map/all_to_all | solution.py:127
  467.2 14.0 %all-to-all-done.11 = bf16[4,128,1024]{2,1,0:T(8,128)(2,1)} async-done(((bf16[4,128,1024]{2,1,0:T(8,128)(2,1)}), bf16[4,128,1024]{2,1,0:T(8,128)(2,1)}, u32[]{:S(2)}, u32[]{:S(2)}) %all-to-all-start.11) | async-done | bytes 1048608 | tf_op jit(solution)/shard_map/all_to_all | solution.py:127
  500.1 11.5 %all-to-all-done.13 = bf16[8,32,4096]{2,1,0:T(8,128)(2,1)S(1)} async-done(((bf16[8,32,4096]{2,1,0:T(8,128)(2,1)}), bf16[8,32,4096]{2,1,0:T(8,128)(2,1)S(1)}, u32[]{:S(2)}, u32[]{:S(2)}) %all-to-all-start.13) | async-done | bytes 2097184 | tf_op jit(solution)/shard_map/all_to_all | solution.py:110
  (151 shorter events, 177.1 us)
Async XLA Ops:
  7.2 191.6 %copy-start = (bf16[1,16,768]{2,1,0:T(8,128)(2,1)S(1)}, bf16[1,16,768]{2,1,0:T(8,128)(2,1)}, u32[]{:S(2)}) copy-start(bf16[1,16,768]{2,1,0:T(8,128)(2,1)} %param.26) | copy-start | bytes 73732
  7.2 33.5 %all-gather.8.cloned.1.call-start = ((), (), s32[]{:S(2)}) async-start(), calls=%async_computation.15 | async-start | bytes 1310720 | tf_op jit(solution)/shard_map/all_gather | solution.py:67
  44.8 37.7 %all-to-all-start = ((bf16[8,144,1024]{2,1,0:T(8,128)(2,1)}), bf16[8,144,1024]{2,1,0:T(8,128)(2,1)S(1)}, u32[]{:S(2)}, u32[]{:S(2)}) async-start(bf16[8,144,1024]{2,1,0:T(8,128)(2,1)} %multiply_convert_fusion.3), calls=%async_computation | async-start | bytes 4718592 | tf_op jit(solution)/shard_map/all_to_all | solution.py:70
  48.5 30.1 %all-gather.10.cloned.1.call-start = ((), (), s32[]{:S(2)}) async-start(), calls=%async_computation.16 | async-start | bytes 1310720 | tf_op jit(solution)/shard_map/all_gather | solution.py:67
  49.2 58.3 %all-gather.12.cloned.1.call-start = ((), (), s32[]{:S(2)}) async-start(), calls=%async_computation.17 | async-start | bytes 1310720 | tf_op jit(solution)/shard_map/all_gather | solution.py:67
  82.6 33.8 %all-to-all-start.1 = ((bf16[8,144,1024]{2,1,0:T(8,128)(2,1)}), bf16[8,144,1024]{2,1,0:T(8,128)(2,1)}, u32[]{:S(2)}, u32[]{:S(2)}) async-start(bf16[8,144,1024]{2,1,0:T(8,128)(2,1)} %multiply_convert_fusion.2), calls=%async_computation.1 | async-start | bytes 4718592 | tf_op jit(solution)/shard_map/all_to_all | solution.py:70
  86.9 50.1 %all-gather.14.cloned.1.call-start = ((), (), s32[]{:S(2)}) async-start(), calls=%async_computation.18 | async-start | bytes 1310720 | tf_op jit(solution)/shard_map/all_gather | solution.py:67
  116.4 35.0 %all-to-all-start.2 = ((bf16[8,144,1024]{2,1,0:T(8,128)(2,1)}), bf16[8,144,1024]{2,1,0:T(8,128)(2,1)}, u32[]{:S(2)}, u32[]{:S(2)}) async-start(bf16[8,144,1024]{2,1,0:T(8,128)(2,1)} %multiply_convert_fusion.1), calls=%async_computation.2 | async-start | bytes 4718592 | tf_op jit(solution)/shard_map/all_to_all | solution.py:70
  120.8 203.3 %all-gather.18.cloned.1.call-start = ((), (), s32[]{:S(2)}) async-start(), calls=%async_computation.20 | async-start | bytes 2359296 | tf_op jit(solution)/shard_map/all_gather | solution.py:73
  121.6 19.4 %copy-start.11 = (bf16[1,16,4096]{2,1,0:T(8,128)(2,1)S(1)}, bf16[1,16,4096]{2,1,0:T(8,128)(2,1)}, u32[]{:S(2)}) copy-start(bf16[1,16,4096]{2,1,0:T(8,128)(2,1)} %param.27) | copy-start | bytes 393220
  151.4 39.5 %all-to-all-start.3 = ((bf16[8,144,1024]{2,1,0:T(8,128)(2,1)}), bf16[8,144,1024]{2,1,0:T(8,128)(2,1)}, u32[]{:S(2)}, u32[]{:S(2)}) async-start(bf16[8,144,1024]{2,1,0:T(8,128)(2,1)} %multiply_convert_fusion), calls=%async_computation.3 | async-start | bytes 4718592 | tf_op jit(solution)/shard_map/all_to_all | solution.py:70
  203.9 13.4 %all-to-all-start.12 = ((bf16[8,144,32]{1,2,0:T(8,128)(2,1)}), bf16[8,144,32]{1,2,0:T(8,128)(2,1)S(1)}, u32[]{:S(2)}, u32[]{:S(2)}) async-start(bf16[8,144,32]{1,2,0:T(8,128)(2,1)} %copy.31), calls=%async_computation.12 | async-start | bytes 262144 | tf_op jit(solution)/shard_map/all_to_all | solution.py:105
  217.9 33.8 %all-to-all-start.4 = ((bf16[8,144,1024]{2,1,0:T(8,128)(2,1)}), bf16[8,144,1024]{2,1,0:T(8,128)(2,1)}, u32[]{:S(2)}, u32[]{:S(2)}) async-start(bf16[8,144,1024]{2,1,0:T(8,128)(2,1)} %bitcast.214), calls=%async_computation.4 | async-start | bytes 4718592 | tf_op jit(solution)/shard_map/all_to_all | solution.py:123
  222.3 101.8 %all-gather.16.cloned.1.call-start = ((), (), s32[]{:S(2)}) async-start(), calls=%async_computation.19 | async-start | bytes 5242880 | tf_op jit(solution)/shard_map/all_gather | solution.py:74
  251.8 33.8 %all-to-all-start.6 = ((bf16[8,144,1024]{2,1,0:T(8,128)(2,1)}), bf16[8,144,1024]{2,1,0:T(8,128)(2,1)}, u32[]{:S(2)}, u32[]{:S(2)}) async-start(bf16[8,144,1024]{2,1,0:T(8,128)(2,1)} %bitcast.216), calls=%async_computation.6 | async-start | bytes 4718592 | tf_op jit(solution)/shard_map/all_to_all | solution.py:123
  285.6 34.1 %all-to-all-start.8 = ((bf16[8,144,1024]{2,1,0:T(8,128)(2,1)}), bf16[8,144,1024]{2,1,0:T(8,128)(2,1)}, u32[]{:S(2)}, u32[]{:S(2)}) async-start(bf16[8,144,1024]{2,1,0:T(8,128)(2,1)} %bitcast.215), calls=%async_computation.8 | async-start | bytes 4718592 | tf_op jit(solution)/shard_map/all_to_all | solution.py:123
  319.7 33.8 %all-to-all-start.10 = ((bf16[8,144,1024]{2,1,0:T(8,128)(2,1)}), bf16[8,144,1024]{2,1,0:T(8,128)(2,1)}, u32[]{:S(2)}, u32[]{:S(2)}) async-start(bf16[8,144,1024]{2,1,0:T(8,128)(2,1)} %bitcast.213), calls=%async_computation.10 | async-start | bytes 4718592 | tf_op jit(solution)/shard_map/all_to_all | solution.py:123
  353.5 8.8 %all-to-all-start.14 = ((bf16[8,144,32]{1,2,0:T(8,128)(2,1)}), bf16[8,144,32]{1,2,0:T(8,128)(2,1)S(1)}, u32[]{:S(2)}, u32[]{:S(2)}) async-start(bf16[8,144,32]{1,2,0:T(8,128)(2,1)} %fusion.79), calls=%async_computation.14 | async-start | bytes 262144 | tf_op jit(solution)/shard_map/all_to_all | solution.py:77
  363.0 29.3 %all-to-all-start.5 = ((bf16[4,128,1024]{2,1,0:T(8,128)(2,1)}), bf16[4,128,1024]{2,1,0:T(8,128)(2,1)S(1)}, u32[]{:S(2)}, u32[]{:S(2)}) async-start(bf16[4,128,1024]{2,1,0:T(8,128)(2,1)} %bitcast.220), calls=%async_computation.5 | async-start | bytes 2097152 | tf_op jit(solution)/shard_map/all_to_all | solution.py:127
  392.3 29.5 %all-to-all-start.7 = ((bf16[4,128,1024]{2,1,0:T(8,128)(2,1)}), bf16[4,128,1024]{2,1,0:T(8,128)(2,1)}, u32[]{:S(2)}, u32[]{:S(2)}) async-start(bf16[4,128,1024]{2,1,0:T(8,128)(2,1)} %bitcast.221), calls=%async_computation.7 | async-start | bytes 2097152 | tf_op jit(solution)/shard_map/all_to_all | solution.py:127
  421.9 29.8 %all-to-all-start.9 = ((bf16[4,128,1024]{2,1,0:T(8,128)(2,1)}), bf16[4,128,1024]{2,1,0:T(8,128)(2,1)}, u32[]{:S(2)}, u32[]{:S(2)}) async-start(bf16[4,128,1024]{2,1,0:T(8,128)(2,1)} %bitcast.219), calls=%async_computation.9 | async-start | bytes 2097152 | tf_op jit(solution)/shard_map/all_to_all | solution.py:127
  451.7 29.5 %all-to-all-start.11 = ((bf16[4,128,1024]{2,1,0:T(8,128)(2,1)}), bf16[4,128,1024]{2,1,0:T(8,128)(2,1)}, u32[]{:S(2)}, u32[]{:S(2)}) async-start(bf16[4,128,1024]{2,1,0:T(8,128)(2,1)} %bitcast.218), calls=%async_computation.11 | async-start | bytes 2097152 | tf_op jit(solution)/shard_map/all_to_all | solution.py:127
  467.2 18.4 %copy-start.17 = (bf16[1152,16]{0,1:T(8,128)(2,1)S(1)}, bf16[1152,16]{0,1:T(8,128)(2,1)}, u32[]{:S(2)}) copy-start(bf16[1152,16]{0,1:T(8,128)(2,1)} %copy-done.16) | copy-start | bytes 110596
  481.2 30.3 %all-to-all-start.13 = ((bf16[8,32,4096]{2,1,0:T(8,128)(2,1)}), bf16[8,32,4096]{2,1,0:T(8,128)(2,1)S(1)}, u32[]{:S(2)}, u32[]{:S(2)}) async-start(bf16[8,32,4096]{2,1,0:T(8,128)(2,1)} %bitcast.217), calls=%async_computation.13 | async-start | bytes 4194304 | tf_op jit(solution)/shard_map/all_to_all | solution.py:110
  (24 other events, 123.8 us)
Sparse Core Ops, SparseCore 0:
  9.6 31.0 all-gather.7
  50.9 27.6 all-gather.9
  80.1 27.4 all-gather.11
  109.6 27.4 all-gather.13
  138.8 32.8 all-gather.17
  224.4 80.5 all-gather.15

commit v2 on v1

v2 whole, which is shorter than its diff:
```python
import jax
import jax.numpy as jnp
from jax import lax
from jax.sharding import PartitionSpec as P

scale = 2.0
bf, f32, i32 = jnp.bfloat16, jnp.float32, jnp.int32


def dot(a, b, da, db):
    return lax.dot_general(
        a, b, (((da,), (db,)), ((), ())), preferred_element_type=jnp.float32
    )


def swap(pieces, nc):
    got = [pieces[0]]
    for j in range(1, nc):
        got.append(lax.ppermute(pieces[j], "ctx", [(c, c ^ j) for c in range(nc)]))
    return got


def one_hot(index, size):
    return (index[..., None] == jnp.arange(size, dtype=i32)).astype(bf)


def local(
    x,
    grad,
    ids,
    weights,
    gate_w,
    up_w,
    down_w,
    gate_in,
    gate_out,
    up_in,
    up_out,
    down_in,
    down_out,
    gate_pre,
    up_pre,
):
    gate_w, up_w, down_w = gate_w[0], up_w[0], down_w[0]
    gate_in, gate_out, up_in, up_out = gate_in[0], gate_out[0], up_in[0], up_out[0]
    down_in, down_out, gate_pre, up_pre = down_in[0], down_out[0], gate_pre[0], up_pre[0]
    tok, width = x.shape
    rank = gate_in.shape[0]
    nc, ne = lax.axis_size("ctx"), lax.axis_size("ep")
    slots = gate_pre.shape[0]
    rows = slots // nc
    cap = rows // ne
    part = slots // ne
    fold = ne
    cols = width // fold
    top = ids.shape[1]
    col, me = lax.axis_index("ctx"), lax.axis_index("ep")
    near = col ^ jnp.arange(nc, dtype=i32)

    def from_next(value, step):
        return lax.ppermute(value, "ep", [((e + step) % ne, e) for e in range(ne)])

    stacked = jnp.concatenate([grad[:, h * cols : (h + 1) * cols] for h in range(fold)], axis=0)
    packed = jnp.concatenate([ids.astype(f32), weights], axis=1)
    metas, grads, xs = [packed], [stacked], [x]
    for k in range(1, ne):
        metas.append(from_next(packed, k))
    for k in range(1, ne):
        grads.append(from_next(grads[-1], 1))
    for k in range(1, ne):
        xs.append(from_next(xs[-1], 1))

    both_in = jnp.concatenate([gate_in, up_in], axis=0)
    both_all = lax.all_gather(both_in, "ctx")[near].reshape(nc * 2 * rank, width)
    scaled_in = (both_in.astype(f32) * scale).astype(bf)

    mine = near * ne + me
    iota = jnp.arange(tok, dtype=i32)
    lower = (iota[:, None] > iota[None, :]).astype(bf)
    fold_iota = jnp.arange(fold, dtype=i32) * cap
    flat = jnp.arange(part, dtype=i32)
    flat_j, flat_s = flat // cap, flat % cap
    stack_of = [one_hot(flat_j * fold * cap + h * cap + flat_s, nc * fold * cap) for h in range(fold)]
    long = jnp.arange(slots, dtype=i32)
    unstack = one_hot(
        (long // cap) % fold * part + (long // (fold * cap)) * cap + long % cap, slots
    )
    down_grad = [0.0] * fold
    down_in_grad = 0.0

    keys, picks, hiddens, backs, gates, ups, returns = [], [], [], [], [], [], []
    for k in range(ne):
        chosen = metas[k][:, :top].astype(i32)
        hit = chosen[:, :, None] == mine[None, None, :]
        sel = jnp.any(hit, axis=1)
        wt = jnp.sum(jnp.where(hit, metas[k][:, top:, None], 0.0), axis=1).T
        place = dot(lower, sel.astype(bf), 1, 0).astype(i32).T
        key = jnp.where(sel.T, place, -slots)
        keys.append(key)
        key_h = (key[:, None, :] + fold_iota[None, :, None]).reshape(nc, 1, fold * tok)
        wt_h = jnp.broadcast_to(wt[:, None, :], (nc, fold, tok)).reshape(nc, 1, fold * tok)
        match = key_h == jnp.arange(fold * cap, dtype=i32)[None, :, None]
        pick = match.astype(bf)
        picks.append(pick)
        slot_w = jnp.sum(jnp.where(match, wt_h, 0.0), axis=2, keepdims=True)
        sent = [(dot(pick[j], grads[k], 1, 0) * slot_w[j]).astype(bf) for j in range(nc)]
        got = jnp.concatenate(swap(sent, nc), axis=0)
        got = [dot(stack_of[h], got, 1, 0).astype(bf) for h in range(fold)]

        at = near[flat_j] * rows + (me + k) % ne * cap + flat_s
        order = one_hot(at, slots)
        gate_v, up_v = dot(order, gate_pre, 1, 0), dot(order, up_pre, 1, 0)
        sig = jax.nn.sigmoid(gate_v)
        silu = gate_v * sig
        hidden = (silu * up_v).astype(bf)
        down_lora = dot(hidden, down_in, 1, 1).astype(bf)
        grad_lora, grad_hidden = 0.0, 0.0
        for h in range(fold):
            span = slice(h * cols, (h + 1) * cols)
            grad_lora += dot(got[h], down_out[:, span], 1, 1)
            grad_hidden += dot(got[h], down_w[:, span], 1, 1)
            down_grad[h] += dot(down_lora, got[h], 0, 0)
        grad_lora = grad_lora.astype(bf)
        grad_hidden += scale * dot(grad_lora, down_in, 1, 0)
        down_in_grad += dot(grad_lora, hidden, 0, 0)
        grad_gate = (grad_hidden * up_v * sig * (1.0 + gate_v * (1.0 - sig))).astype(bf)
        grad_up = (grad_hidden * silu).astype(bf)
        back = jnp.concatenate(
            [dot(grad_gate, gate_out, 1, 1).astype(bf), dot(grad_up, up_out, 1, 1).astype(bf)], axis=1
        )
        gates.append(grad_gate)
        ups.append(grad_up)
        backs.append(back)
        out = []
        for h in range(fold):
            span = slice(h * cols, (h + 1) * cols)
            out.append(
                (
                    dot(grad_gate, gate_w[span], 1, 1)
                    + dot(grad_up, up_w[span], 1, 1)
                    + dot(back, scaled_in[:, span], 1, 0)
                ).astype(bf)
            )
        out = jnp.concatenate(out, axis=0)
        out = [
            dot(unstack[j * rows : (j + 1) * rows], out, 1, 0).astype(bf) for j in range(nc)
        ]
        returned = jnp.concatenate(swap(out, nc), axis=0)
        partial = dot(pick.reshape(slots, fold * tok), returned, 0, 0)
        if k:
            partial = lax.ppermute(
                partial.astype(bf), "ep", [(e, (e + k) % ne) for e in range(ne)]
            ).astype(f32)
        returns.append(partial)

    total = sum(returns)
    grad_in = jnp.concatenate(
        [total[h * tok : (h + 1) * tok].astype(bf) for h in range(fold)], axis=1
    )

    x_all = jnp.concatenate(xs, axis=0)
    key_k = jnp.stack([keys[k] + k * cap for k in range(ne)], axis=1).reshape(nc, 1, ne * tok)
    pick_k = (key_k == jnp.arange(rows, dtype=i32)[None, :, None]).astype(bf)
    lora_tok = dot(x_all, both_all, 1, 1).astype(bf)
    lora = [
        dot(pick_k[j], lora_tok[:, j * 2 * rank : (j + 1) * 2 * rank], 1, 0).astype(bf)
        for j in range(nc)
    ]
    lora = jnp.concatenate(swap(lora, nc), axis=0).reshape(nc, ne, cap, 2 * rank)
    lora = jnp.transpose(lora, (1, 0, 2, 3)).reshape(slots, 2 * rank)
    gate_all, up_all = jnp.concatenate(gates, axis=0), jnp.concatenate(ups, axis=0)
    gate_output_gradient = (scale * dot(lora[:, :rank], gate_all, 0, 0)).astype(bf)
    up_output_gradient = (scale * dot(lora[:, rank:], up_all, 0, 0)).astype(bf)

    back = jnp.concatenate(backs, axis=0).reshape(ne, nc, cap, 2 * rank)
    back = jnp.transpose(back, (1, 0, 2, 3)).reshape(nc, rows, 2 * rank)
    back = swap([back[j] for j in range(nc)], nc)
    share = [
        scale * dot(dot(back[j], pick_k[j], 0, 0).astype(bf), x_all, 1, 0) for j in range(nc)
    ]
    share = [share[0]] + swap([s.astype(bf) for s in share], nc)[1:]
    both_input_gradients = sum(s.astype(f32) for s in share).astype(bf)
    down_output_gradient = jnp.concatenate([(scale * d).astype(bf) for d in down_grad], axis=1)
    return (
        grad_in,
        both_input_gradients[None, :rank],
        gate_output_gradient[None],
        both_input_gradients[None, rank:],
        up_output_gradient[None],
        (scale * down_in_grad).astype(bf)[None],
        down_output_gradient[None],
    )


def solution(mesh):
    flat, deep = P(("ctx", "ep"), None), P(("ctx", "ep"), None, None)
    return jax.shard_map(
        local,
        mesh=mesh,
        in_specs=(flat,) * 4 + (deep,) * 11,
        out_specs=(flat,) + (deep,) * 6,
        check_vma=False,
    )
```

time: 528 us -> 606 us (1.15)
  the two profiles are of different devices: /device:TPU:0 before, /device:TPU:9 now
where the time goes in v2:
time: 606 us; the launch traced here: 596 us
  waiting for transfers between devices  228 us (38%)
  matrix products  185 us (31%)
  starting transfers between devices  108 us (18%)
  local copies, waits for them, and re-layouts  33.6 us (6%)
  other arithmetic  23 us (4%)
  between operations  17.5 us (3%)
    dot_general x231, matrix products, dot(): lax.dot_general(a, b, (((da,), (db,)), ((), ())), preferred_element_type=...  185 us
    ppermute x77, waiting for transfers between devices, swap(): got.append(lax.ppermute(pieces[j], 'ctx', [(c, c ^ j) for c in range(nc)]))  157 us
    ppermute x77, starting transfers between devices, swap(): got.append(lax.ppermute(pieces[j], 'ctx', [(c, c ^ j) for c in range(nc)]))  94.8 us
    ppermute x3, waiting for transfers between devices, local(): lax.ppermute(partial.astype(bf), 'ep', [(e, (e + k) % ne) for e in range(...  70.7 us
    unnamed x257, local copies, waits for them, and re-layouts  15.9 us
  transfers between devices with their start and end apart: 90, of which 30 were waited for; matrix products, arithmetic and copies ran while one was open for 37% of the time, Pallas kernels for 0%

profile of v2, /device:TPU:9, one launch (start us, length us, event | category | flops | bytes accessed | tf_op | source)
XLA Modules:
  0.0 596.0 jit_solution(7245780804514557703)
XLA Ops:
  20.0 4.6 fusion.488
  53.4 4.4 collective-permute-done.2
  59.9 13.1 %collective-permute-start.6 = (bf16[144,1024]{1,0:T(8,128)(2,1)S(1)}, bf16[144,1024]{1,0:T(8,128)(2,1)S(1)}, u32[]{:S(2)}, u32[]{:S(2)}) collective-permute-start(bf16[144,1024]{1,0:T(8,128)(2,1)S(1)} %fusion.219), channel_id=1, source_target_pairs={{0,28},{4,24},{8,20},{12,16},{16,12},{20,8},{24,4},{28,0},{1,29},{... | collective-permute-start | bytes 884744 | tf_op jit(solution)/shard_map/ppermute | solution.py:19
  73.0 6.1 %collective-permute-done.4 = bf16[144,1024]{1,0:T(8,128)(2,1)S(1)} collective-permute-done((bf16[144,1024]{1,0:T(8,128)(2,1)S(1)}, bf16[144,1024]{1,0:T(8,128)(2,1)S(1)}, u32[]{:S(2)}, u32[]{:S(2)}) %collective-permute-start.4) | collective-permute-done | bytes 294944 | tf_op jit(solution)/shard_map/ppermute | solution.py:19
  109.6 3.9 collective-permute-done.8
  123.1 14.1 %collective-permute-done.11 = bf16[144,1024]{1,0:T(8,128)(2,1)S(1)} collective-permute-done((bf16[144,1024]{1,0:T(8,128)(2,1)S(1)}, bf16[144,1024]{1,0:T(8,128)(2,1)S(1)}, u32[]{:S(2)}, u32[]{:S(2)}) %collective-permute-start.11) | collective-permute-done | bytes 294944 | tf_op jit(solution)/shard_map/ppermute | solution.py:19
  164.1 13.1 %collective-permute-done.20 = bf16[144,1024]{1,0:T(8,128)(2,1)S(1)} collective-permute-done((bf16[144,1024]{1,0:T(8,128)(2,1)S(1)}, bf16[144,1024]{1,0:T(8,128)(2,1)S(1)}, u32[]{:S(2)}, u32[]{:S(2)}) %collective-permute-start.20) | collective-permute-done | bytes 294944 | tf_op jit(solution)/shard_map/ppermute | solution.py:19
  213.8 4.2 collective-permute-done.25
  221.4 6.5 %collective-permute-done.28 = bf16[144,1024]{1,0:T(8,128)(2,1)S(1)} collective-permute-done((bf16[144,1024]{1,0:T(8,128)(2,1)S(1)}, bf16[144,1024]{1,0:T(8,128)(2,1)S(1)}, u32[]{:S(2)}, u32[]{:S(2)}) %collective-permute-start.28) | collective-permute-done | bytes 294944 | tf_op jit(solution)/shard_map/ppermute | solution.py:19
  227.9 6.3 %collective-permute-done.29 = bf16[144,1024]{1,0:T(8,128)(2,1)S(1)} collective-permute-done((bf16[144,1024]{1,0:T(8,128)(2,1)S(1)}, bf16[144,1024]{1,0:T(8,128)(2,1)S(1)}, u32[]{:S(2)}, u32[]{:S(2)}) %collective-permute-start.29) | collective-permute-done | bytes 294944 | tf_op jit(solution)/shard_map/ppermute | solution.py:19
  249.3 4.7 collective-permute-done.35
  256.4 12.3 %collective-permute-done.37 = bf16[144,1024]{1,0:T(8,128)(2,1)S(1)} collective-permute-done((bf16[144,1024]{1,0:T(8,128)(2,1)S(1)}, bf16[144,1024]{1,0:T(8,128)(2,1)S(1)}, u32[]{:S(2)}, u32[]{:S(2)}) %collective-permute-start.37) | collective-permute-done | bytes 294944 | tf_op jit(solution)/shard_map/ppermute | solution.py:19
  295.9 4.9 collective-permute-done.41
  303.8 4.2 collective-permute-done.42
  311.3 6.5 %collective-permute-done.45 = bf16[144,1024]{1,0:T(8,128)(2,1)S(1)} collective-permute-done((bf16[144,1024]{1,0:T(8,128)(2,1)S(1)}, bf16[144,1024]{1,0:T(8,128)(2,1)S(1)}, u32[]{:S(2)}, u32[]{:S(2)}) %collective-permute-start.45) | collective-permute-done | bytes 294944 | tf_op jit(solution)/shard_map/ppermute | solution.py:19
  317.8 6.3 %collective-permute-done.46 = bf16[144,1024]{1,0:T(8,128)(2,1)S(1)} collective-permute-done((bf16[144,1024]{1,0:T(8,128)(2,1)S(1)}, bf16[144,1024]{1,0:T(8,128)(2,1)S(1)}, u32[]{:S(2)}, u32[]{:S(2)}) %collective-permute-start.46) | collective-permute-done | bytes 294944 | tf_op jit(solution)/shard_map/ppermute | solution.py:19
  339.1 4.9 collective-permute-done.52
  344.1 14.3 %collective-permute-done.54 = bf16[144,1024]{1,0:T(8,128)(2,1)S(1)} collective-permute-done((bf16[144,1024]{1,0:T(8,128)(2,1)S(1)}, bf16[144,1024]{1,0:T(8,128)(2,1)S(1)}, u32[]{:S(2)}, u32[]{:S(2)}) %collective-permute-start.54) | collective-permute-done | bytes 294944 | tf_op jit(solution)/shard_map/ppermute | solution.py:19
  411.3 3.9 fusion.9
  426.8 3.9 fusion.13
  438.4 4.2 convolution_convert_fusion.35
  469.9 11.0 %collective-permute-done.61 = bf16[144,1024]{1,0:T(8,128)(2,1)} collective-permute-done((bf16[144,1024]{1,0:T(8,128)(2,1)}, bf16[144,1024]{1,0:T(8,128)(2,1)}, u32[]{:S(2)}, u32[]{:S(2)}) %collective-permute-start.61) | collective-permute-done | bytes 294944 | tf_op jit(solution)/shard_map/ppermute | solution.py:19
  493.2 14.7 %collective-permute-done.77 = bf16[32,4096]{1,0:T(8,128)(2,1)S(1)} collective-permute-done((bf16[32,4096]{1,0:T(8,128)(2,1)S(1)}, bf16[32,4096]{1,0:T(8,128)(2,1)S(1)}, u32[]{:S(2)}, u32[]{:S(2)}) %collective-permute-start.77) | collective-permute-done | bytes 262176 | tf_op jit(solution)/shard_map/ppermute | solution.py:19
  516.0 66.6 %collective-permute-done.47 = bf16[512,1024]{1,0:T(8,128)(2,1)} collective-permute-done((bf16[512,1024]{1,0:T(8,128)(2,1)}, bf16[512,1024]{1,0:T(8,128)(2,1)}, u32[]{:S(2)}, u32[]{:S(2)}) %collective-permute-start.47) | collective-permute-done | bytes 1048608 | tf_op jit(solution)/shard_map/ppermute | solution.py:151
  (739 shorter events, 339.5 us)
Async XLA Ops:
  7.2 427.4 %all-gather.3.cloned.1.call-start = ((), (), s32[]{:S(2)}) async-start(), calls=%async_computation | async-start | bytes 2359296 | tf_op jit(solution)/shard_map/all_gather | solution.py:74
  8.8 27.7 %collective-permute-start.31 = (f32[128,16]{0,1:T(8,128)S(1)}, f32[128,16]{0,1:T(8,128)S(1)}, u32[]{:S(2)}, u32[]{:S(2)}) collective-permute-start(f32[128,16]{0,1:T(8,128)S(1)} %pad_maximum_fusion.11), channel_id=1, source_target_pairs={{2,0},{3,1},{0,2},{1,3},{6,4},{7,5},{4,6},{5,7},{10,8},{11,9},{8,1... | collective-permute-start | bytes 24584 | tf_op jit(solution)/shard_map/ppermute | solution.py:61
  11.1 25.4 %collective-permute-start.48 = (f32[128,16]{0,1:T(8,128)S(1)}, f32[128,16]{0,1:T(8,128)S(1)}, u32[]{:S(2)}, u32[]{:S(2)}) collective-permute-start(f32[128,16]{0,1:T(8,128)S(1)} %pad_maximum_fusion.11), channel_id=1, source_target_pairs={{3,0},{0,1},{1,2},{2,3},{7,4},{4,5},{5,6},{6,7},{11,8},{8,9},{9,10... | collective-permute-start | bytes 24584 | tf_op jit(solution)/shard_map/ppermute | solution.py:61
  11.1 25.4 %collective-permute-start.14 = (f32[128,16]{0,1:T(8,128)S(1)}, f32[128,16]{0,1:T(8,128)S(1)}, u32[]{:S(2)}, u32[]{:S(2)}) collective-permute-start(f32[128,16]{0,1:T(8,128)S(1)} %pad_maximum_fusion.11), channel_id=1, source_target_pairs={{1,0},{2,1},{3,2},{0,3},{5,4},{6,5},{7,6},{4,7},{9,8},{10,9},{11,1... | collective-permute-start | bytes 24584 | tf_op jit(solution)/shard_map/ppermute | solution.py:61
  13.9 126.4 %collective-permute-start.15 = (bf16[512,1024]{1,0:T(8,128)(2,1)S(1)}, bf16[512,1024]{1,0:T(8,128)(2,1)}, u32[]{:S(2)}, u32[]{:S(2)}) collective-permute-start(bf16[512,1024]{1,0:T(8,128)(2,1)S(1)} %pad_maximum_fusion.4), channel_id=1, source_target_pairs={{1,0},{2,1},{3,2},{0,3},{5,4},{6,5},{7,6},{4,7},{9,8},{10,9},{11,1... | collective-permute-start | bytes 3145736 | tf_op jit(solution)/shard_map/ppermute | solution.py:61
  15.9 137.4 %collective-permute-start.65 = (bf16[128,4096]{1,0:T(8,128)(2,1)}, bf16[128,4096]{1,0:T(8,128)(2,1)}, u32[]{:S(2)}, u32[]{:S(2)}) collective-permute-start(bf16[128,4096]{1,0:T(8,128)(2,1)} %param.15), channel_id=1, source_target_pairs={{1,0},{2,1},{3,2},{0,3},{5,4},{6,5},{7,6},{4,7},{9,8},{10,9},{11,1... | collective-permute-start | bytes 3145736 | tf_op jit(solution)/shard_map/ppermute | solution.py:61
  52.8 26.4 %collective-permute-start.4 = (bf16[144,1024]{1,0:T(8,128)(2,1)S(1)}, bf16[144,1024]{1,0:T(8,128)(2,1)S(1)}, u32[]{:S(2)}, u32[]{:S(2)}) collective-permute-start(bf16[144,1024]{1,0:T(8,128)(2,1)S(1)} %fusion.217), channel_id=1, source_target_pairs={{0,20},{4,16},{8,28},{12,24},{16,4},{20,0},{24,12},{28,8},{1,21},{... | collective-permute-start | bytes 884744 | tf_op jit(solution)/shard_map/ppermute | solution.py:19
  113.5 23.7 %collective-permute-start.11 = (bf16[144,1024]{1,0:T(8,128)(2,1)S(1)}, bf16[144,1024]{1,0:T(8,128)(2,1)S(1)}, u32[]{:S(2)}, u32[]{:S(2)}) collective-permute-start(bf16[144,1024]{1,0:T(8,128)(2,1)S(1)} %convolution_convert_fusion.29), channel_id=1, source_target_pairs={{0,20},{4,16},{8,28},{12,24},{16,4},{20,0},{24,12},{28,8},{1,21},{... | collective-permute-start | bytes 884744 | tf_op jit(solution)/shard_map/ppermute | solution.py:19
  153.3 23.9 %collective-permute-start.20 = (bf16[144,1024]{1,0:T(8,128)(2,1)S(1)}, bf16[144,1024]{1,0:T(8,128)(2,1)S(1)}, u32[]{:S(2)}, u32[]{:S(2)}) collective-permute-start(bf16[144,1024]{1,0:T(8,128)(2,1)S(1)} %fusion.226), channel_id=1, source_target_pairs={{0,20},{4,16},{8,28},{12,24},{16,4},{20,0},{24,12},{28,8},{1,21},{... | collective-permute-start | bytes 884744 | tf_op jit(solution)/shard_map/ppermute | solution.py:19
  161.4 75.5 %collective-permute-start.32 = (bf16[512,1024]{1,0:T(8,128)(2,1)}, bf16[512,1024]{1,0:T(8,128)(2,1)S(1)}, u32[]{:S(2)}, u32[]{:S(2)}) collective-permute-start(bf16[512,1024]{1,0:T(8,128)(2,1)} %collective-permute-done.15), channel_id=1, source_target_pairs={{1,0},{2,1},{3,2},{0,3},{5,4},{6,5},{7,6},{4,7},{9,8},{10,9},{11,1... | collective-permute-start | bytes 3145736 | tf_op jit(solution)/shard_map/ppermute | solution.py:61
  161.8 80.4 %collective-permute-start.66 = (bf16[128,4096]{1,0:T(8,128)(2,1)}, bf16[128,4096]{1,0:T(8,128)(2,1)S(1)}, u32[]{:S(2)}, u32[]{:S(2)}) collective-permute-start(bf16[128,4096]{1,0:T(8,128)(2,1)} %collective-permute-done.65), channel_id=1, source_target_pairs={{1,0},{2,1},{3,2},{0,3},{5,4},{6,5},{7,6},{4,7},{9,8},{10,9},{11,1... | collective-permute-start | bytes 3145736 | tf_op jit(solution)/shard_map/ppermute | solution.py:61
  242.2 26.5 %collective-permute-start.37 = (bf16[144,1024]{1,0:T(8,128)(2,1)S(1)}, bf16[144,1024]{1,0:T(8,128)(2,1)S(1)}, u32[]{:S(2)}, u32[]{:S(2)}) collective-permute-start(bf16[144,1024]{1,0:T(8,128)(2,1)S(1)} %fusion.235), channel_id=1, source_target_pairs={{0,20},{4,16},{8,28},{12,24},{16,4},{20,0},{24,12},{28,8},{1,21},{... | collective-permute-start | bytes 884744 | tf_op jit(solution)/shard_map/ppermute | solution.py:19
  244.0 24.8 %collective-permute-start.38 = (bf16[144,1024]{1,0:T(8,128)(2,1)S(1)}, bf16[144,1024]{1,0:T(8,128)(2,1)S(1)}, u32[]{:S(2)}, u32[]{:S(2)}) collective-permute-start(bf16[144,1024]{1,0:T(8,128)(2,1)S(1)} %fusion.236), channel_id=1, source_target_pairs={{0,24},{4,28},{8,16},{12,20},{16,8},{20,12},{24,0},{28,4},{1,25},{... | collective-permute-start | bytes 884744 | tf_op jit(solution)/shard_map/ppermute | solution.py:19
  254.0 72.7 %collective-permute-start.49 = (bf16[512,1024]{1,0:T(8,128)(2,1)S(1)}, bf16[512,1024]{1,0:T(8,128)(2,1)S(1)}, u32[]{:S(2)}, u32[]{:S(2)}) collective-permute-start(bf16[512,1024]{1,0:T(8,128)(2,1)S(1)} %collective-permute-done.32), channel_id=1, source_target_pairs={{1,0},{2,1},{3,2},{0,3},{5,4},{6,5},{7,6},{4,7},{9,8},{10,9},{11,1... | collective-permute-start | bytes 3145736 | tf_op jit(solution)/shard_map/ppermute | solution.py:61
  254.4 77.7 %collective-permute-start.67 = (bf16[128,4096]{1,0:T(8,128)(2,1)S(1)}, bf16[128,4096]{1,0:T(8,128)(2,1)}, u32[]{:S(2)}, u32[]{:S(2)}) collective-permute-start(bf16[128,4096]{1,0:T(8,128)(2,1)S(1)} %collective-permute-done.66), channel_id=1, source_target_pairs={{1,0},{2,1},{3,2},{0,3},{5,4},{6,5},{7,6},{4,7},{9,8},{10,9},{11,1... | collective-permute-start | bytes 3145736 | tf_op jit(solution)/shard_map/ppermute | solution.py:61
  332.0 26.4 %collective-permute-start.54 = (bf16[144,1024]{1,0:T(8,128)(2,1)S(1)}, bf16[144,1024]{1,0:T(8,128)(2,1)S(1)}, u32[]{:S(2)}, u32[]{:S(2)}) collective-permute-start(bf16[144,1024]{1,0:T(8,128)(2,1)S(1)} %fusion.244), channel_id=1, source_target_pairs={{0,20},{4,16},{8,28},{12,24},{16,4},{20,0},{24,12},{28,8},{1,21},{... | collective-permute-start | bytes 884744 | tf_op jit(solution)/shard_map/ppermute | solution.py:19
  335.3 23.1 %collective-permute-start.55 = (bf16[144,1024]{1,0:T(8,128)(2,1)S(1)}, bf16[144,1024]{1,0:T(8,128)(2,1)S(1)}, u32[]{:S(2)}, u32[]{:S(2)}) collective-permute-start(bf16[144,1024]{1,0:T(8,128)(2,1)S(1)} %fusion.245), channel_id=1, source_target_pairs={{0,24},{4,28},{8,16},{12,20},{16,8},{20,12},{24,0},{28,4},{1,25},{... | collective-permute-start | bytes 884744 | tf_op jit(solution)/shard_map/ppermute | solution.py:19
  453.3 27.6 %collective-permute-start.61 = (bf16[144,1024]{1,0:T(8,128)(2,1)}, bf16[144,1024]{1,0:T(8,128)(2,1)}, u32[]{:S(2)}, u32[]{:S(2)}) collective-permute-start(bf16[144,1024]{1,0:T(8,128)(2,1)} %convolution_convert_fusion.5), channel_id=1, source_target_pairs={{0,20},{4,16},{8,28},{12,24},{16,4},{20,0},{24,12},{28,8},{1,21},{... | collective-permute-start | bytes 884744 | tf_op jit(solution)/shard_map/ppermute | solution.py:19
  483.5 24.4 %collective-permute-start.77 = (bf16[32,4096]{1,0:T(8,128)(2,1)S(1)}, bf16[32,4096]{1,0:T(8,128)(2,1)S(1)}, u32[]{:S(2)}, u32[]{:S(2)}) collective-permute-start(bf16[32,4096]{1,0:T(8,128)(2,1)S(1)} %copy-done.27), channel_id=1, source_target_pairs={{0,20},{4,16},{8,28},{12,24},{16,4},{20,0},{24,12},{28,8},{1,21},{... | collective-permute-start | bytes 786440 | tf_op jit(solution)/shard_map/ppermute | solution.py:19
  484.8 23.5 %collective-permute-start.79 = (bf16[32,4096]{1,0:T(8,128)(2,1)S(1)}, bf16[32,4096]{1,0:T(8,128)(2,1)S(1)}, u32[]{:S(2)}, u32[]{:S(2)}) collective-permute-start(bf16[32,4096]{1,0:T(8,128)(2,1)S(1)} %copy-done.26), channel_id=1, source_target_pairs={{0,24},{4,28},{8,16},{12,20},{16,8},{20,12},{24,0},{28,4},{1,25},{... | collective-permute-start | bytes 786440 | tf_op jit(solution)/shard_map/ppermute | solution.py:19
  486.0 23.3 %collective-permute-start.81 = (bf16[32,4096]{1,0:T(8,128)(2,1)S(1)}, bf16[32,4096]{1,0:T(8,128)(2,1)}, u32[]{:S(2)}, u32[]{:S(2)}) collective-permute-start(bf16[32,4096]{1,0:T(8,128)(2,1)S(1)} %copy-done.28), channel_id=1, source_target_pairs={{0,28},{4,24},{8,20},{12,16},{16,12},{20,8},{24,4},{28,0},{1,29},{... | collective-permute-start | bytes 786440 | tf_op jit(solution)/shard_map/ppermute | solution.py:19
  490.8 25.2 %collective-permute-start.30 = (bf16[512,1024]{1,0:T(8,128)(2,1)}, bf16[512,1024]{1,0:T(8,128)(2,1)S(1)}, u32[]{:S(2)}, u32[]{:S(2)}) collective-permute-start(bf16[512,1024]{1,0:T(8,128)(2,1)} %convolution_convert_fusion.2), channel_id=1, source_target_pairs={{0,1},{1,2},{2,3},{3,0},{4,5},{5,6},{6,7},{7,4},{8,9},{9,10},{10,1... | collective-permute-start | bytes 3145736 | tf_op jit(solution)/shard_map/ppermute | solution.py:151
  492.2 90.3 %collective-permute-start.47 = (bf16[512,1024]{1,0:T(8,128)(2,1)}, bf16[512,1024]{1,0:T(8,128)(2,1)}, u32[]{:S(2)}, u32[]{:S(2)}) collective-permute-start(bf16[512,1024]{1,0:T(8,128)(2,1)} %convolution_convert_fusion.1), channel_id=1, source_target_pairs={{0,2},{1,3},{2,0},{3,1},{4,6},{5,7},{6,4},{7,5},{8,10},{9,11},{10,... | collective-permute-start | bytes 3145736 | tf_op jit(solution)/shard_map/ppermute | solution.py:151
  507.9 76.7 %collective-permute-start.64 = (bf16[512,1024]{1,0:T(8,128)(2,1)}, bf16[512,1024]{1,0:T(8,128)(2,1)}, u32[]{:S(2)}, u32[]{:S(2)}) collective-permute-start(bf16[512,1024]{1,0:T(8,128)(2,1)} %convolution_convert_fusion), channel_id=1, source_target_pairs={{0,3},{1,0},{2,1},{3,2},{4,7},{5,4},{6,5},{7,6},{8,11},{9,8},{10,9... | collective-permute-start | bytes 3145736 | tf_op jit(solution)/shard_map/ppermute | solution.py:151
  (169 other events, 2161.9 us)
Sparse Core Ops, SparseCore 0:
  16.8 31.4 all-gather.2

commit v3 on v2

v3 whole, which is shorter than its diff:
```python
import jax
import jax.numpy as jnp
from jax import lax
from jax.sharding import PartitionSpec as P

scale = 2.0
bf, f32, i32 = jnp.bfloat16, jnp.float32, jnp.int32


def dot(a, b, da, db):
    return lax.dot_general(
        a, b, (((da,), (db,)), ((), ())), preferred_element_type=jnp.float32
    )


def swap(value, col):
    nc = value.shape[0]
    near = col ^ jnp.arange(nc, dtype=i32)
    out = value[near]
    got = [out[0]]
    for j in range(1, nc):
        got.append(lax.ppermute(out[j], "ctx", [(c, c ^ j) for c in range(nc)]))
    return jnp.stack(got)[near]


def one_hot(index, size):
    return (index[..., None] == jnp.arange(size, dtype=i32)).astype(bf)


def local(
    x,
    grad,
    ids,
    weights,
    gate_w,
    up_w,
    down_w,
    gate_in,
    gate_out,
    up_in,
    up_out,
    down_in,
    down_out,
    gate_pre,
    up_pre,
):
    gate_w, up_w, down_w = gate_w[0], up_w[0], down_w[0]
    gate_in, gate_out, up_in, up_out = gate_in[0], gate_out[0], up_in[0], up_out[0]
    down_in, down_out, gate_pre, up_pre = down_in[0], down_out[0], gate_pre[0], up_pre[0]
    tok, width = x.shape
    rank = gate_in.shape[0]
    nc, ne = lax.axis_size("ctx"), lax.axis_size("ep")
    slots = gate_pre.shape[0]
    rows = slots // nc
    cap = rows // ne
    part = slots // ne
    fold = ne
    cols = width // fold
    top = ids.shape[1]
    col, me = lax.axis_index("ctx"), lax.axis_index("ep")

    def from_next(value, step):
        return lax.ppermute(value, "ep", [((e + step) % ne, e) for e in range(ne)])

    stacked = jnp.concatenate([grad[:, h * cols : (h + 1) * cols] for h in range(fold)], axis=0)
    packed = jnp.concatenate([ids.astype(f32), weights], axis=1)
    metas = [packed] + [from_next(packed, k) for k in range(1, ne)]
    mine = jnp.arange(nc, dtype=i32) * ne + me
    iota = jnp.arange(tok, dtype=i32)
    lower = (iota[:, None] > iota[None, :]).astype(bf)
    fold_iota = jnp.arange(fold, dtype=i32) * cap

    def build(k, block):
        chosen = metas[k][:, :top].astype(i32)
        hit = chosen[:, :, None] == mine[None, None, :]
        sel = jnp.any(hit, axis=1)
        wt = jnp.sum(jnp.where(hit, metas[k][:, top:, None], 0.0), axis=1).T
        place = dot(lower, sel.astype(bf), 1, 0).astype(i32).T
        key = jnp.where(sel.T, place, -slots)
        key_h = (key[:, None, :] + fold_iota[None, :, None]).reshape(nc, 1, fold * tok)
        wt_h = jnp.broadcast_to(wt[:, None, :], (nc, fold, tok)).reshape(nc, 1, fold * tok)
        match = key_h == jnp.arange(rows, dtype=i32)[None, :, None]
        pick = match.astype(bf)
        slot_w = jnp.sum(jnp.where(match, wt_h, 0.0), axis=2, keepdims=True)
        return key, pick, (dot(pick, block, 2, 0) * slot_w).astype(bf)

    def exchange(value):
        return lax.all_to_all(value, "ctx", split_axis=0, concat_axis=0, tiled=True)

    keys, picks, gots, blocks = [], [], [], [stacked]
    for k in range(ne):
        if k:
            blocks.append(from_next(blocks[-1], 1))
        key, pick, sent = build(k, blocks[k])
        if k:
            sent, gots[-1] = lax.optimization_barrier((sent, gots[-1]))
        keys.append(key)
        picks.append(pick)
        gots.append(exchange(sent))
        if k == 0:
            first = sent
    flat = jnp.arange(part, dtype=i32)
    long = jnp.arange(slots, dtype=i32)
    flat, long, gate_pre, up_pre, first = lax.optimization_barrier(
        (flat, long, gate_pre, up_pre, first)
    )
    both_in = jnp.concatenate([gate_in, up_in], axis=0)
    both_all = lax.all_gather(both_in, "ctx", tiled=True)
    scaled_in = (both_in.astype(f32) * scale).astype(bf)
    late_x, _ = lax.optimization_barrier((x, blocks[-1]))
    xs = [x] + [from_next(late_x, k) for k in range(1, ne)]

    flat_j, flat_s = flat // cap, flat % cap
    stack_of = [one_hot(flat_j * rows + h * cap + flat_s, slots) for h in range(fold)]
    unstack = one_hot((long // cap) % fold * part + (long // rows) * cap + long % cap, slots)
    down_grad = [0.0] * fold
    down_in_grad = 0.0
    backs, gates, ups, outs = [], [], [], []
    for k in range(ne):
        order = one_hot(flat_j * rows + (me + k) % ne * cap + flat_s, slots)
        gate_v, up_v = dot(order, gate_pre, 1, 0), dot(order, up_pre, 1, 0)
        sig = jax.nn.sigmoid(gate_v)
        silu = gate_v * sig
        hidden = (silu * up_v).astype(bf)
        down_lora = dot(hidden, down_in, 1, 1).astype(bf)
        pieces = gots[k].reshape(slots, cols)
        got = [dot(stack_of[h], pieces, 1, 0).astype(bf) for h in range(fold)]
        grad_lora, grad_hidden = 0.0, 0.0
        for h in range(fold):
            span = slice(h * cols, (h + 1) * cols)
            grad_lora += dot(got[h], down_out[:, span], 1, 1)
            grad_hidden += dot(got[h], down_w[:, span], 1, 1)
            down_grad[h] += dot(down_lora, got[h], 0, 0)
        grad_lora = grad_lora.astype(bf)
        grad_hidden += scale * dot(grad_lora, down_in, 1, 0)
        down_in_grad += dot(grad_lora, hidden, 0, 0)
        grad_gate = (grad_hidden * up_v * sig * (1.0 + gate_v * (1.0 - sig))).astype(bf)
        grad_up = (grad_hidden * silu).astype(bf)
        back = jnp.concatenate(
            [dot(grad_gate, gate_out, 1, 1).astype(bf), dot(grad_up, up_out, 1, 1).astype(bf)], axis=1
        )
        gates.append(grad_gate)
        ups.append(grad_up)
        backs.append(back)
        out = []
        for h in range(fold):
            span = slice(h * cols, (h + 1) * cols)
            out.append(
                (
                    dot(grad_gate, gate_w[span], 1, 1)
                    + dot(grad_up, up_w[span], 1, 1)
                    + dot(back, scaled_in[:, span], 1, 0)
                ).astype(bf)
            )
        out = jnp.concatenate(out, axis=0)
        outs.append(dot(unstack, out, 1, 0).astype(bf).reshape(nc, rows, cols))

    total, before = 0.0, gots[-1]
    for k in list(range(1, ne)) + [0]:
        out, _ = lax.optimization_barrier((outs[k], before))
        before = exchange(out)
        partial = dot(picks[k].reshape(slots, fold * tok), before.reshape(slots, cols), 0, 0)
        if k:
            partial = lax.ppermute(
                partial.astype(bf), "ep", [(e, (e + k) % ne) for e in range(ne)]
            ).astype(f32)
        total = total + partial
    grad_in = jnp.concatenate(
        [total[h * tok : (h + 1) * tok].astype(bf) for h in range(fold)], axis=1
    )

    x_all = jnp.concatenate(xs, axis=0)
    key_k = jnp.stack([keys[k] + k * cap for k in range(ne)], axis=1).reshape(nc, 1, ne * tok)
    pick_k = (key_k == jnp.arange(rows, dtype=i32)[None, :, None]).astype(bf)
    lora_tok = dot(x_all, both_all, 1, 1).astype(bf).reshape(ne * tok, nc, 2 * rank)
    lora = jnp.einsum("jrt,tji->jri", pick_k, lora_tok, preferred_element_type=f32).astype(bf)
    lora = swap(lora, col).reshape(nc, ne, cap, 2 * rank)
    lora = jnp.transpose(lora, (1, 0, 2, 3)).reshape(slots, 2 * rank)
    gate_all, up_all = jnp.concatenate(gates, axis=0), jnp.concatenate(ups, axis=0)
    gate_output_gradient = (scale * dot(lora[:, :rank], gate_all, 0, 0)).astype(bf)
    up_output_gradient = (scale * dot(lora[:, rank:], up_all, 0, 0)).astype(bf)

    back = jnp.concatenate(backs, axis=0).reshape(ne, nc, cap, 2 * rank)
    back = swap(jnp.transpose(back, (1, 0, 2, 3)).reshape(nc, rows, 2 * rank), col)
    spread = jnp.einsum("jri,jrt->jit", back, pick_k, preferred_element_type=f32).astype(bf)
    share = scale * dot(spread.reshape(nc * 2 * rank, ne * tok), x_all, 1, 0)
    both_input_gradients = lax.psum_scatter(share, "ctx", scatter_dimension=0, tiled=True).astype(bf)
    down_output_gradient = jnp.concatenate([(scale * d).astype(bf) for d in down_grad], axis=1)
    return (
        grad_in,
        both_input_gradients[None, :rank],
        gate_output_gradient[None],
        both_input_gradients[None, rank:],
        up_output_gradient[None],
        (scale * down_in_grad).astype(bf)[None],
        down_output_gradient[None],
    )


def solution(mesh):
    flat, deep = P(("ctx", "ep"), None), P(("ctx", "ep"), None, None)
    return jax.shard_map(
        local,
        mesh=mesh,
        in_specs=(flat,) * 4 + (deep,) * 11,
        out_specs=(flat,) + (deep,) * 6,
        check_vma=False,
    )
```

time: 606 us -> 596 us (0.983)
  the two profiles are of different devices: /device:TPU:9 before, /device:TPU:11 now
where the time goes in v3:
time: 596 us; the launch traced here: 588 us
  matrix products  241 us (40%)
  waiting for transfers between devices  187 us (31%)
  starting transfers between devices  81.9 us (14%)
  local copies, waits for them, and re-layouts  51.1 us (9%)
  between operations  16.8 us (3%)
  other arithmetic  9.7 us (2%)
    dot_general x160, matrix products, dot(): lax.dot_general(a, b, (((da,), (db,)), ((), ())), preferred_element_type=...  238 us
    all_to_all x8, waiting for transfers between devices, exchange(): return lax.all_to_all(value, 'ctx', split_axis=0, concat_axis=0, tiled=True)  64.6 us
    ppermute x3, waiting for transfers between devices, local(): lax.ppermute(partial.astype(bf), 'ep', [(e, (e + k) % ne) for e in range(...  59.5 us
    all_to_all x8, starting transfers between devices, exchange(): return lax.all_to_all(value, 'ctx', split_axis=0, concat_axis=0, tiled=True)  50.8 us
    ppermute x9, waiting for transfers between devices, from_next(): return lax.ppermute(value, 'ep', [((e + step) % ne, e) for e in range(ne)])  44.6 us
    unnamed x299, local copies, waits for them, and re-layouts  24.2 us
    ppermute x14, waiting for transfers between devices, swap(): got.append(lax.ppermute(out[j], 'ctx', [(c, c ^ j) for c in range(nc)]))  18.4 us
    ppermute x14, starting transfers between devices, swap(): got.append(lax.ppermute(out[j], 'ctx', [(c, c ^ j) for c in range(nc)]))  14.4 us
  transfers between devices with their start and end apart: 36, of which 11 were waited for; matrix products, arithmetic and copies ran while one was open for 40% of the time, Pallas kernels for 0%

profile of v3, /device:TPU:11, one launch (start us, length us, event | category | flops | bytes accessed | tf_op | source)
XLA Modules:
  0.0 587.6 jit_solution(1225252909438101856)
XLA Ops:
  24.3 6.2 %all-to-all-start = ((bf16[8,144,1024]{2,1,0:T(8,128)(2,1)}), bf16[8,144,1024]{2,1,0:T(8,128)(2,1)}, u32[]{:S(2)}, u32[]{:S(2)}) async-start(bf16[8,144,1024]{2,1,0:T(8,128)(2,1)} %multiply_convert_fusion.3), calls=%async_computation | async-start | bytes 4718592 | tf_op jit(solution)/shard_map/all_to_all | solution.py:88
  45.3 18.9 %all-to-all-done = bf16[8,144,1024]{2,1,0:T(8,128)(2,1)} async-done(((bf16[8,144,1024]{2,1,0:T(8,128)(2,1)}), bf16[8,144,1024]{2,1,0:T(8,128)(2,1)}, u32[]{:S(2)}, u32[]{:S(2)}) %all-to-all-start) | async-done | bytes 2359328 | tf_op jit(solution)/shard_map/all_to_all | solution.py:88
  90.0 6.3 %all-to-all-start.1 = ((bf16[8,144,1024]{2,1,0:T(8,128)(2,1)}), bf16[8,144,1024]{2,1,0:T(8,128)(2,1)}, u32[]{:S(2)}, u32[]{:S(2)}) async-start(bf16[8,144,1024]{2,1,0:T(8,128)(2,1)} %multiply_convert_fusion.1), calls=%async_computation.1 | async-start | bytes 4718592 | tf_op jit(solution)/shard_map/all_to_all | solution.py:88
  108.5 4.8 fusion.7
  117.3 14.9 %collective-permute-done.5 = bf16[512,1024]{1,0:T(8,128)(2,1)S(1)} collective-permute-done((bf16[512,1024]{1,0:T(8,128)(2,1)}, bf16[512,1024]{1,0:T(8,128)(2,1)S(1)}, u32[]{:S(2)}, u32[]{:S(2)}) %collective-permute-start.5) | collective-permute-done | bytes 1048608 | tf_op jit(solution)/shard_map/ppermute | solution.py:63
  164.7 6.5 %all-to-all-start.2 = ((bf16[8,144,1024]{2,1,0:T(8,128)(2,1)}), bf16[8,144,1024]{2,1,0:T(8,128)(2,1)}, u32[]{:S(2)}, u32[]{:S(2)}) async-start(bf16[8,144,1024]{2,1,0:T(8,128)(2,1)} %multiply_convert_fusion.2), calls=%async_computation.2 | async-start | bytes 4718592 | tf_op jit(solution)/shard_map/all_to_all | solution.py:88
  181.0 4.7 fusion.4
  191.7 9.6 %collective-permute-done.17 = bf16[128,4096]{1,0:T(8,128)(2,1)} collective-permute-done((bf16[128,4096]{1,0:T(8,128)(2,1)}, bf16[128,4096]{1,0:T(8,128)(2,1)}, u32[]{:S(2)}, u32[]{:S(2)}) %collective-permute-start.17) | collective-permute-done | bytes 1048608 | tf_op jit(solution)/shard_map/ppermute | solution.py:63
  203.6 20.1 %collective-permute-done.18 = bf16[128,4096]{1,0:T(8,128)(2,1)} collective-permute-done((bf16[128,4096]{1,0:T(8,128)(2,1)}, bf16[128,4096]{1,0:T(8,128)(2,1)}, u32[]{:S(2)}, u32[]{:S(2)}) %collective-permute-start.18) | collective-permute-done | bytes 1048608 | tf_op jit(solution)/shard_map/ppermute | solution.py:63
  277.9 5.4 all-to-all-start.3
  304.6 4.8 fusion.5
  358.6 5.5 all-to-all-start.4
  373.7 18.0 %collective-permute-done.14 = bf16[144,32]{0,1:T(8,128)(2,1)S(1)} collective-permute-done((bf16[144,32]{0,1:T(8,128)(2,1)}, bf16[144,32]{0,1:T(8,128)(2,1)S(1)}, u32[]{:S(2)}, u32[]{:S(2)}) %collective-permute-start.14) | collective-permute-done | bytes 9248 | tf_op jit(solution)/shard_map/ppermute | solution.py:22
  397.0 5.5 convolution_multiply_fusion
  408.1 6.7 %all-to-all-start.5 = ((bf16[8,144,1024]{2,1,0:T(8,128)(2,1)}), bf16[8,144,1024]{2,1,0:T(8,128)(2,1)}, u32[]{:S(2)}, u32[]{:S(2)}) async-start(bf16[8,144,1024]{2,1,0:T(8,128)(2,1)} %bitcast.494), calls=%async_computation.5 | async-start | bytes 4718592 | tf_op jit(solution)/shard_map/all_to_all | solution.py:88
  423.6 4.7 fusion.6
  428.3 23.3 %all-to-all-done.5 = bf16[8,144,1024]{2,1,0:T(8,128)(2,1)} async-done(((bf16[8,144,1024]{2,1,0:T(8,128)(2,1)}), bf16[8,144,1024]{2,1,0:T(8,128)(2,1)}, u32[]{:S(2)}, u32[]{:S(2)}) %all-to-all-start.5) | async-done | bytes 2359328 | tf_op jit(solution)/shard_map/all_to_all | solution.py:88
  451.7 8.3 %all-to-all-start.6 = ((bf16[8,144,1024]{2,1,0:T(8,128)(2,1)}), bf16[8,144,1024]{2,1,0:T(8,128)(2,1)}, u32[]{:S(2)}, u32[]{:S(2)}) async-start(bf16[8,144,1024]{2,1,0:T(8,128)(2,1)} %bitcast.495), calls=%async_computation.6 | async-start | bytes 4718592 | tf_op jit(solution)/shard_map/all_to_all | solution.py:88
  473.1 20.5 %all-to-all-done.6 = bf16[8,144,1024]{2,1,0:T(8,128)(2,1)} async-done(((bf16[8,144,1024]{2,1,0:T(8,128)(2,1)}), bf16[8,144,1024]{2,1,0:T(8,128)(2,1)}, u32[]{:S(2)}, u32[]{:S(2)}) %all-to-all-start.6) | async-done | bytes 2359328 | tf_op jit(solution)/shard_map/all_to_all | solution.py:88
  493.5 6.0 %all-to-all-start.7 = ((bf16[8,144,1024]{2,1,0:T(8,128)(2,1)}), bf16[8,144,1024]{2,1,0:T(8,128)(2,1)}, u32[]{:S(2)}, u32[]{:S(2)}) async-start(bf16[8,144,1024]{2,1,0:T(8,128)(2,1)} %bitcast.492), calls=%async_computation.7 | async-start | bytes 4718592 | tf_op jit(solution)/shard_map/all_to_all | solution.py:88
  499.5 4.3 bitcast_convert_fusion.1
  503.8 4.2 bitcast_convert_fusion
  515.6 56.0 %collective-permute-done.7 = bf16[512,1024]{1,0:T(8,128)(2,1)} collective-permute-done((bf16[512,1024]{1,0:T(8,128)(2,1)}, bf16[512,1024]{1,0:T(8,128)(2,1)}, u32[]{:S(2)}, u32[]{:S(2)}) %collective-permute-start.7) | collective-permute-done | bytes 1048608 | tf_op jit(solution)/shard_map/ppermute | solution.py:164
  575.1 4.2 fusion.50
  (577 shorter events, 301.5 us)
Async XLA Ops:
  7.2 218.8 %all-gather.2.cloned.1.call-start = ((), (), s32[]{:S(2)}) async-start(), calls=%async_computation.10 | async-start | bytes 2359296 | tf_op jit(solution)/shard_map/all_gather | solution.py:108
  14.8 26.2 %collective-permute-start.2 = (bf16[512,1024]{1,0:T(8,128)(2,1)}, bf16[512,1024]{1,0:T(8,128)(2,1)}, u32[]{:S(2)}, u32[]{:S(2)}) collective-permute-start(bf16[512,1024]{1,0:T(8,128)(2,1)} %pad_maximum_fusion), channel_id=1, source_target_pairs={{1,0},{2,1},{3,2},{0,3},{5,4},{6,5},{7,6},{4,7},{9,8},{10,9},{11,1... | collective-permute-start | bytes 3145736 | tf_op jit(solution)/shard_map/ppermute | solution.py:63
  24.3 39.8 %all-to-all-start = ((bf16[8,144,1024]{2,1,0:T(8,128)(2,1)}), bf16[8,144,1024]{2,1,0:T(8,128)(2,1)}, u32[]{:S(2)}, u32[]{:S(2)}) async-start(bf16[8,144,1024]{2,1,0:T(8,128)(2,1)} %multiply_convert_fusion.3), calls=%async_computation | async-start | bytes 4718592 | tf_op jit(solution)/shard_map/all_to_all | solution.py:88
  41.0 66.6 %collective-permute-start.3 = (bf16[512,1024]{1,0:T(8,128)(2,1)}, bf16[512,1024]{1,0:T(8,128)(2,1)}, u32[]{:S(2)}, u32[]{:S(2)}) collective-permute-start(bf16[512,1024]{1,0:T(8,128)(2,1)} %collective-permute-done.2), channel_id=1, source_target_pairs={{1,0},{2,1},{3,2},{0,3},{5,4},{6,5},{7,6},{4,7},{9,8},{10,9},{11,1... | collective-permute-start | bytes 3145736 | tf_op jit(solution)/shard_map/ppermute | solution.py:63
  90.0 49.6 %all-to-all-start.1 = ((bf16[8,144,1024]{2,1,0:T(8,128)(2,1)}), bf16[8,144,1024]{2,1,0:T(8,128)(2,1)}, u32[]{:S(2)}, u32[]{:S(2)}) async-start(bf16[8,144,1024]{2,1,0:T(8,128)(2,1)} %multiply_convert_fusion.1), calls=%async_computation.1 | async-start | bytes 4718592 | tf_op jit(solution)/shard_map/all_to_all | solution.py:88
  107.6 24.6 %collective-permute-start.5 = (bf16[512,1024]{1,0:T(8,128)(2,1)}, bf16[512,1024]{1,0:T(8,128)(2,1)S(1)}, u32[]{:S(2)}, u32[]{:S(2)}) collective-permute-start(bf16[512,1024]{1,0:T(8,128)(2,1)} %collective-permute-done.3), channel_id=1, source_target_pairs={{1,0},{2,1},{3,2},{0,3},{5,4},{6,5},{7,6},{4,7},{9,8},{10,9},{11,1... | collective-permute-start | bytes 3145736 | tf_op jit(solution)/shard_map/ppermute | solution.py:63
  132.2 57.2 %collective-permute-start.16 = (bf16[128,4096]{1,0:T(8,128)(2,1)}, bf16[128,4096]{1,0:T(8,128)(2,1)}, u32[]{:S(2)}, u32[]{:S(2)}) collective-permute-start(bf16[128,4096]{1,0:T(8,128)(2,1)} %param.15), channel_id=1, source_target_pairs={{1,0},{2,1},{3,2},{0,3},{5,4},{6,5},{7,6},{4,7},{9,8},{10,9},{11,1... | collective-permute-start | bytes 3145736 | tf_op jit(solution)/shard_map/ppermute | solution.py:63
  132.6 68.7 %collective-permute-start.17 = (bf16[128,4096]{1,0:T(8,128)(2,1)}, bf16[128,4096]{1,0:T(8,128)(2,1)}, u32[]{:S(2)}, u32[]{:S(2)}) collective-permute-start(bf16[128,4096]{1,0:T(8,128)(2,1)} %param.15), channel_id=1, source_target_pairs={{2,0},{3,1},{0,2},{1,3},{6,4},{7,5},{4,6},{5,7},{10,8},{11,9},{8,1... | collective-permute-start | bytes 3145736 | tf_op jit(solution)/shard_map/ppermute | solution.py:63
  134.0 89.7 %collective-permute-start.18 = (bf16[128,4096]{1,0:T(8,128)(2,1)}, bf16[128,4096]{1,0:T(8,128)(2,1)}, u32[]{:S(2)}, u32[]{:S(2)}) collective-permute-start(bf16[128,4096]{1,0:T(8,128)(2,1)} %param.15), channel_id=1, source_target_pairs={{3,0},{0,1},{1,2},{2,3},{7,4},{4,5},{5,6},{6,7},{11,8},{8,9},{9,10... | collective-permute-start | bytes 3145736 | tf_op jit(solution)/shard_map/ppermute | solution.py:63
  164.7 88.3 %all-to-all-start.2 = ((bf16[8,144,1024]{2,1,0:T(8,128)(2,1)}), bf16[8,144,1024]{2,1,0:T(8,128)(2,1)}, u32[]{:S(2)}, u32[]{:S(2)}) async-start(bf16[8,144,1024]{2,1,0:T(8,128)(2,1)} %multiply_convert_fusion.2), calls=%async_computation.2 | async-start | bytes 4718592 | tf_op jit(solution)/shard_map/all_to_all | solution.py:88
  277.9 33.4 %all-to-all-start.3 = ((bf16[8,144,1024]{2,1,0:T(8,128)(2,1)}), bf16[8,144,1024]{2,1,0:T(8,128)(2,1)}, u32[]{:S(2)}, u32[]{:S(2)}) async-start(bf16[8,144,1024]{2,1,0:T(8,128)(2,1)} %multiply_convert_fusion), calls=%async_computation.3 | async-start | bytes 4718592 | tf_op jit(solution)/shard_map/all_to_all | solution.py:88
  344.8 19.3 %collective-permute-start.9 = (bf16[144,32]{0,1:T(8,128)(2,1)}, bf16[144,32]{0,1:T(8,128)(2,1)}, u32[]{:S(2)}, u32[]{:S(2)}) collective-permute-start(bf16[144,32]{0,1:T(8,128)(2,1)} %get-tuple-element.83), channel_id=1, source_target_pairs={{0,4},{4,0},{8,12},{12,8},{16,20},{20,16},{24,28},{28,24},{1,5},{5... | collective-permute-start | bytes 27656 | tf_op jit(solution)/shard_map/ppermute | solution.py:22
  356.9 14.2 %collective-permute-start.12 = (bf16[144,32]{0,1:T(8,128)(2,1)}, bf16[144,32]{0,1:T(8,128)(2,1)}, u32[]{:S(2)}, u32[]{:S(2)}) collective-permute-start(bf16[144,32]{0,1:T(8,128)(2,1)} %get-tuple-element.80), channel_id=1, source_target_pairs={{0,16},{4,20},{8,24},{12,28},{16,0},{20,4},{24,8},{28,12},{1,17},{... | collective-permute-start | bytes 27656 | tf_op jit(solution)/shard_map/ppermute | solution.py:22
  357.2 15.2 %collective-permute-start.13 = (bf16[144,32]{0,1:T(8,128)(2,1)}, bf16[144,32]{0,1:T(8,128)(2,1)}, u32[]{:S(2)}, u32[]{:S(2)}) collective-permute-start(bf16[144,32]{0,1:T(8,128)(2,1)} %get-tuple-element.79), channel_id=1, source_target_pairs={{0,20},{4,16},{8,28},{12,24},{16,4},{20,0},{24,12},{28,8},{1,21},{... | collective-permute-start | bytes 27656 | tf_op jit(solution)/shard_map/ppermute | solution.py:22
  358.6 49.5 %all-to-all-start.4 = ((bf16[8,144,1024]{2,1,0:T(8,128)(2,1)}), bf16[8,144,1024]{2,1,0:T(8,128)(2,1)}, u32[]{:S(2)}, u32[]{:S(2)}) async-start(bf16[8,144,1024]{2,1,0:T(8,128)(2,1)} %bitcast.493), calls=%async_computation.4 | async-start | bytes 4718592 | tf_op jit(solution)/shard_map/all_to_all | solution.py:88
  364.1 149.7 %reduce-scatter.2.cloned.1.call-start = ((), (), s32[]{:S(2)}) async-start(), calls=%async_computation.9 | async-start | bytes 4718592 | tf_op jit(solution)/shard_map/reduce_scatter | solution.py:187
  364.1 27.6 %collective-permute-start.14 = (bf16[144,32]{0,1:T(8,128)(2,1)}, bf16[144,32]{0,1:T(8,128)(2,1)S(1)}, u32[]{:S(2)}, u32[]{:S(2)}) collective-permute-start(bf16[144,32]{0,1:T(8,128)(2,1)} %get-tuple-element.78), channel_id=1, source_target_pairs={{0,24},{4,28},{8,16},{12,20},{16,8},{20,12},{24,0},{28,4},{1,25},{... | collective-permute-start | bytes 27656 | tf_op jit(solution)/shard_map/ppermute | solution.py:22
  366.7 25.9 %collective-permute-start.15 = (bf16[144,32]{0,1:T(8,128)(2,1)S(1)}, bf16[144,32]{0,1:T(8,128)(2,1)S(1)}, u32[]{:S(2)}, u32[]{:S(2)}) collective-permute-start(bf16[144,32]{0,1:T(8,128)(2,1)S(1)} %get-tuple-element.77), channel_id=1, source_target_pairs={{0,28},{4,24},{8,20},{12,16},{16,12},{20,8},{24,4},{28,0},{1,29},{... | collective-permute-start | bytes 27656 | tf_op jit(solution)/shard_map/ppermute | solution.py:22
  408.1 43.6 %all-to-all-start.5 = ((bf16[8,144,1024]{2,1,0:T(8,128)(2,1)}), bf16[8,144,1024]{2,1,0:T(8,128)(2,1)}, u32[]{:S(2)}, u32[]{:S(2)}) async-start(bf16[8,144,1024]{2,1,0:T(8,128)(2,1)} %bitcast.494), calls=%async_computation.5 | async-start | bytes 4718592 | tf_op jit(solution)/shard_map/all_to_all | solution.py:88
  451.7 41.9 %all-to-all-start.6 = ((bf16[8,144,1024]{2,1,0:T(8,128)(2,1)}), bf16[8,144,1024]{2,1,0:T(8,128)(2,1)}, u32[]{:S(2)}, u32[]{:S(2)}) async-start(bf16[8,144,1024]{2,1,0:T(8,128)(2,1)} %bitcast.495), calls=%async_computation.6 | async-start | bytes 4718592 | tf_op jit(solution)/shard_map/all_to_all | solution.py:88
  470.9 44.7 %collective-permute-start.6 = (bf16[512,1024]{1,0:T(8,128)(2,1)}, bf16[512,1024]{1,0:T(8,128)(2,1)}, u32[]{:S(2)}, u32[]{:S(2)}) collective-permute-start(bf16[512,1024]{1,0:T(8,128)(2,1)} %bitcast_convert_fusion.2), channel_id=1, source_target_pairs={{0,1},{1,2},{2,3},{3,0},{4,5},{5,6},{6,7},{7,4},{8,9},{9,10},{10,1... | collective-permute-start | bytes 3145736 | tf_op jit(solution)/shard_map/ppermute | solution.py:164
  493.5 81.6 %all-to-all-start.7 = ((bf16[8,144,1024]{2,1,0:T(8,128)(2,1)}), bf16[8,144,1024]{2,1,0:T(8,128)(2,1)}, u32[]{:S(2)}, u32[]{:S(2)}) async-start(bf16[8,144,1024]{2,1,0:T(8,128)(2,1)} %bitcast.492), calls=%async_computation.7 | async-start | bytes 4718592 | tf_op jit(solution)/shard_map/all_to_all | solution.py:88
  503.8 67.8 %collective-permute-start.7 = (bf16[512,1024]{1,0:T(8,128)(2,1)}, bf16[512,1024]{1,0:T(8,128)(2,1)}, u32[]{:S(2)}, u32[]{:S(2)}) collective-permute-start(bf16[512,1024]{1,0:T(8,128)(2,1)} %bitcast_convert_fusion.1), channel_id=1, source_target_pairs={{0,2},{1,3},{2,0},{3,1},{4,6},{5,7},{6,4},{7,5},{8,10},{9,11},{10,... | collective-permute-start | bytes 3145736 | tf_op jit(solution)/shard_map/ppermute | solution.py:164
  508.1 67.0 %collective-permute-start.8 = (bf16[512,1024]{1,0:T(8,128)(2,1)}, bf16[512,1024]{1,0:T(8,128)(2,1)}, u32[]{:S(2)}, u32[]{:S(2)}) collective-permute-start(bf16[512,1024]{1,0:T(8,128)(2,1)} %bitcast_convert_fusion), channel_id=1, source_target_pairs={{0,3},{1,0},{2,1},{3,2},{4,7},{5,4},{6,5},{7,6},{8,11},{9,8},{10,9... | collective-permute-start | bytes 3145736 | tf_op jit(solution)/shard_map/ppermute | solution.py:164
  (154 other events, 2109.6 us)
Sparse Core Ops, SparseCore 0:
  17.7 47.7 all-gather.1
  402.6 78.6 reduce-scatter.1

commit v4 on v1

v4 whole, which is shorter than its diff:
```python
import jax
import jax.numpy as jnp
from jax import lax
from jax.sharding import PartitionSpec as P

scale = 2.0
dispatch_shares = (2, 3, 5, 6)
return_shares = (4, 5, 4, 3)
bf, f32, i32 = jnp.bfloat16, jnp.float32, jnp.int32


def dot(a, b, da, db):
    return lax.dot_general(
        a, b, (((da,), (db,)), ((), ())), preferred_element_type=jnp.float32
    )


def swap(value, col):
    nc = value.shape[0]
    near = col ^ jnp.arange(nc, dtype=i32)
    out = value[near]
    got = [out[0]]
    for j in range(1, nc):
        got.append(lax.ppermute(out[j], "ctx", [(c, c ^ j) for c in range(nc)]))
    return jnp.stack(got)[near]


def spans(width, shares):
    unit, at = width // sum(shares), 0
    for share in shares:
        yield slice(at * unit, (at + share) * unit)
        at += share


def local(
    x,
    grad,
    ids,
    weights,
    gate_w,
    up_w,
    down_w,
    gate_in,
    gate_out,
    up_in,
    up_out,
    down_in,
    down_out,
    gate_pre,
    up_pre,
):
    gate_w, up_w, down_w = gate_w[0], up_w[0], down_w[0]
    gate_in, gate_out, up_in, up_out = gate_in[0], gate_out[0], up_in[0], up_out[0]
    down_in, down_out, gate_pre, up_pre = down_in[0], down_out[0], gate_pre[0], up_pre[0]
    tok, width = x.shape
    rank = gate_in.shape[0]
    nc, ne = lax.axis_size("ctx"), lax.axis_size("ep")
    slots = gate_pre.shape[0]
    rows = slots // nc
    cap = rows // ne
    top = ids.shape[1]
    col, me = lax.axis_index("ctx"), lax.axis_index("ep")

    def hop(value, step):
        return lax.ppermute(value, "ep", [((e + step) % ne, e) for e in range(ne)])

    def exchange(value):
        return lax.all_to_all(value, "ctx", split_axis=0, concat_axis=0, tiled=True)

    packed = jnp.concatenate([ids.astype(f32), weights], axis=1)
    metas = [packed] + [hop(packed, k) for k in range(1, ne)]
    blocks, after = [], None
    for span in spans(width, dispatch_shares):
        own = grad[:, span]
        if after is not None:
            own, _ = lax.optimization_barrier((own, after))
        blocks.append([own] + [hop(own, k) for k in range(1, ne)])
        after = own

    metas = jnp.stack(metas)
    mine = jnp.arange(nc, dtype=i32) * ne + me
    chosen = metas[:, :, :top].astype(i32)
    hit = chosen[:, :, None, :] == mine[None, None, :, None]
    sel = jnp.any(hit, axis=3)
    wt = jnp.sum(jnp.where(hit, metas[:, :, None, top:], 0.0), axis=3)
    iota = jnp.arange(tok, dtype=i32)
    lower = (iota[:, None] > iota[None, :]).astype(bf)
    place = jnp.einsum("ts,esc->cet", lower, sel.astype(bf), preferred_element_type=f32)
    block_of = (me + jnp.arange(ne, dtype=i32)) % ne
    key = place.astype(i32) + (block_of * cap)[None, :, None]
    key = jnp.where(jnp.transpose(sel, (2, 0, 1)), key, -1).reshape(nc, 1, ne * tok)
    wt = jnp.transpose(wt, (2, 0, 1)).reshape(nc, 1, ne * tok)
    match = key == jnp.arange(rows, dtype=i32)[None, :, None]
    pick = match.astype(bf)
    slot_w = jnp.sum(jnp.where(match, wt, 0.0), axis=2, keepdims=True)

    got = []
    for parts in blocks:
        sent = (dot(pick, jnp.concatenate(parts, axis=0), 2, 0) * slot_w).astype(bf)
        if got:
            sent, got[-1] = lax.optimization_barrier((sent, got[-1]))
        got.append(exchange(sent))
    got = [g.reshape(slots, -1) for g in got]
    both_in = jnp.concatenate([gate_in, up_in], axis=0)
    late_x, late_in, _ = lax.optimization_barrier((x, both_in, tuple(blocks[-1])))
    x_all = lax.all_gather(late_x, "ep", tiled=True)
    both_all = lax.all_gather(late_in, "ctx", tiled=True)

    gate_v, up_v = gate_pre.astype(f32), up_pre.astype(f32)
    sig = jax.nn.sigmoid(gate_v)
    silu = gate_v * sig
    hidden = (silu * up_v).astype(bf)
    down_lora = dot(hidden, down_in, 1, 1).astype(bf)
    grad_lora, grad_hidden, down_grad = 0.0, 0.0, []
    for g, span in zip(got, spans(width, dispatch_shares)):
        grad_lora += dot(g, down_out[:, span], 1, 1)
        grad_hidden += dot(g, down_w[:, span], 1, 1)
        down_grad.append((scale * dot(down_lora, g, 0, 0)).astype(bf))
    grad_lora = grad_lora.astype(bf)
    grad_hidden += scale * dot(grad_lora, down_in, 1, 0)
    grad_gate = (grad_hidden * up_v * sig * (1.0 + gate_v * (1.0 - sig))).astype(bf)
    grad_up = (grad_hidden * silu).astype(bf)
    gate_back = dot(grad_gate, gate_out, 1, 1).astype(bf)
    up_back = dot(grad_up, up_out, 1, 1).astype(bf)
    back = jnp.concatenate([gate_back, up_back], axis=1)
    scaled_in = (both_in.astype(f32) * scale).astype(bf)

    grad_in, before = [], None
    for span in spans(width, return_shares):
        rows_out = (
            dot(grad_gate, gate_w[span], 1, 1)
            + dot(grad_up, up_w[span], 1, 1)
            + dot(back, scaled_in[:, span], 1, 0)
        ).astype(bf)
        if before is not None:
            rows_out, _ = lax.optimization_barrier((rows_out, before))
        before = exchange(rows_out.reshape(nc, rows, -1))
        returned = before.reshape(slots, -1)
        total = 0.0
        for k in list(range(1, ne)) + [0]:
            piece = pick[:, :, k * tok : (k + 1) * tok].reshape(slots, tok)
            partial = dot(piece, returned, 0, 0)
            total += hop(partial.astype(bf), ne - k).astype(f32) if k else partial
        grad_in.append(total.astype(bf))
    grad_in = jnp.concatenate(grad_in, axis=1)

    lora_tok = dot(x_all, both_all, 1, 1).astype(bf).reshape(ne, tok, nc, 2 * rank)
    lora_tok = lora_tok[block_of].reshape(ne * tok, nc, 2 * rank)
    lora = jnp.einsum("jrt,tji->jri", pick, lora_tok, preferred_element_type=f32).astype(bf)
    lora = swap(lora, col).reshape(slots, 2 * rank)
    gate_output_gradient = (scale * dot(lora[:, :rank], grad_gate, 0, 0)).astype(bf)
    up_output_gradient = (scale * dot(lora[:, rank:], grad_up, 0, 0)).astype(bf)

    back = swap(back.reshape(nc, rows, 2 * rank), col)
    spread = jnp.einsum("jri,jrt->jit", back, pick, preferred_element_type=f32).astype(bf)
    spread = spread.reshape(nc * 2 * rank, ne, tok)[:, (jnp.arange(ne, dtype=i32) - me) % ne]
    share = scale * dot(spread.reshape(nc * 2 * rank, ne * tok), x_all, 1, 0)
    both_input_gradients = lax.psum_scatter(share, "ctx", scatter_dimension=0, tiled=True).astype(bf)
    return (
        grad_in,
        both_input_gradients[None, :rank],
        gate_output_gradient[None],
        both_input_gradients[None, rank:],
        up_output_gradient[None],
        (scale * dot(grad_lora, hidden, 0, 0)).astype(bf)[None],
        jnp.concatenate(down_grad, axis=1)[None],
    )


def solution(mesh):
    flat, deep = P(("ctx", "ep"), None), P(("ctx", "ep"), None, None)
    return jax.shard_map(
        local,
        mesh=mesh,
        in_specs=(flat,) * 4 + (deep,) * 11,
        out_specs=(flat,) + (deep,) * 6,
        check_vma=False,
    )
```

time: 528 us -> 530 us (level)
  waiting for transfers between devices: 283 us -> 197 us
  starting transfers between devices: 62.3 us -> 148 us
  blocking collectives: 14.9 us -> 0 us
  local copies, waits for them, and re-layouts: 6.14 us -> 15.6 us
  matrix products: 131 us -> 137 us
    all_to_all x15 -> x8, waiting for transfers between devices: 201 us -> 32.3 us  [exchange(): return lax.all_to_all(value, 'ctx', split_axis=0, concat_axis=0, tiled=True)]
    ppermute x0 -> x41, waiting for transfers between devices: none -> 165 us  [the longest x27 111 us: hop(): return lax.ppermute(value, 'ep', [((e + step) % ne, e) for e in range(ne)])]
    ppermute x0 -> x41, starting transfers between devices: none -> 115 us  [the longest x27 102 us: hop(): return lax.ppermute(value, 'ep', [((e + step) % ne, e) for e in range(ne)])]
    all_gather x6 -> x2, waiting for transfers between devices: 79.5 us -> 0.01 us  [the longest x1 0.01 us: local(): both_all = lax.all_gather(late_in, 'ctx', tiled=True)]
    all_to_all x15 -> x8, starting transfers between devices: 62 us -> 32.4 us  [exchange(): return lax.all_to_all(value, 'ctx', split_axis=0, concat_axis=0, tiled=True)]
    all_gather x1 -> x0, blocking collectives: 14.9 us -> none  [local(): packed = lax.all_gather(packed, 'ep')]
    dot_general x41 -> x53, matrix products: 129 us -> 134 us  [dot(): lax.dot_general(a, b, (((da,), (db,)), ((), ())), preferred_element_type=...]
  transfers between devices with their start and end apart: 21 -> 52, of which waited for: 17 -> 20; matrix products, arithmetic and copies ran while one was open for 26% -> 23% of each run, Pallas kernels for 0% -> 0%
where the time goes in v4:
time: 530 us; the launch traced here: 521 us
  waiting for transfers between devices  197 us (37%)
  starting transfers between devices  148 us (28%)
  matrix products  137 us (26%)
  local copies, waits for them, and re-layouts  15.6 us (3%)
  between operations  15 us (3%)
  other arithmetic  8.36 us (2%)
    dot_general x53, matrix products, dot(): lax.dot_general(a, b, (((da,), (db,)), ((), ())), preferred_element_type=...  134 us
    ppermute x27, waiting for transfers between devices, hop(): return lax.ppermute(value, 'ep', [((e + step) % ne, e) for e in range(ne)])  111 us
    ppermute x27, starting transfers between devices, hop(): return lax.ppermute(value, 'ep', [((e + step) % ne, e) for e in range(ne)])  102 us
    ppermute x14, waiting for transfers between devices, swap(): got.append(lax.ppermute(out[j], 'ctx', [(c, c ^ j) for c in range(nc)]))  53.7 us
    all_to_all x8, starting transfers between devices, exchange(): return lax.all_to_all(value, 'ctx', split_axis=0, concat_axis=0, tiled=True)  32.4 us
    all_to_all x8, waiting for transfers between devices, exchange(): return lax.all_to_all(value, 'ctx', split_axis=0, concat_axis=0, tiled=True)  32.3 us
    ppermute x14, starting transfers between devices, swap(): got.append(lax.ppermute(out[j], 'ctx', [(c, c ^ j) for c in range(nc)]))  13.1 us
  transfers between devices with their start and end apart: 52, of which 20 were waited for; matrix products, arithmetic and copies ran while one was open for 23% of the time, Pallas kernels for 0%

profile of v4, /device:TPU:0, one launch (start us, length us, event | category | flops | bytes accessed | tf_op | source)
XLA Modules:
  0.0 520.9 jit_solution(17698069526487732838)
XLA Ops:
  19.9 6.5 %collective-permute-done.14 = bf16[128,1536]{1,0:T(8,128)(2,1)S(1)} collective-permute-done((bf16[128,1536]{1,0:T(8,128)(2,1)S(1)}, bf16[128,1536]{1,0:T(8,128)(2,1)S(1)}, u32[]{:S(2)}, u32[]{:S(2)}) %collective-permute-start.14) | collective-permute-done | bytes 393248 | tf_op jit(solution)/shard_map/ppermute | solution.py:65
  26.3 16.0 %collective-permute-done.13 = bf16[128,1536]{1,0:T(8,128)(2,1)S(1)} collective-permute-done((bf16[128,1536]{1,0:T(8,128)(2,1)S(1)}, bf16[128,1536]{1,0:T(8,128)(2,1)S(1)}, u32[]{:S(2)}, u32[]{:S(2)}) %collective-permute-start.13) | collective-permute-done | bytes 393248 | tf_op jit(solution)/shard_map/ppermute | solution.py:65
  42.5 7.9 %collective-permute-start.1 = (f32[128,16]{0,1:T(8,128)S(1)}, f32[128,16]{0,1:T(8,128)S(1)}, u32[]{:S(2)}, u32[]{:S(2)}) collective-permute-start(f32[128,16]{0,1:T(8,128)S(1)} %get-tuple-element.58), channel_id=1, source_target_pairs={{2,0},{3,1},{0,2},{1,3},{6,4},{7,5},{4,6},{5,7},{10,8},{11,9},{8,1... | collective-permute-start | bytes 24584 | tf_op jit(solution)/shard_map/ppermute | solution.py:65
  81.8 8.2 %collective-permute-done.4 = bf16[128,768]{1,0:T(8,128)(2,1)S(1)} collective-permute-done((bf16[128,768]{1,0:T(8,128)(2,1)S(1)}, bf16[128,768]{1,0:T(8,128)(2,1)S(1)}, u32[]{:S(2)}, u32[]{:S(2)}) %collective-permute-start.4) | collective-permute-done | bytes 196640 | tf_op jit(solution)/shard_map/ppermute | solution.py:65
  101.2 42.0 %collective-permute-done.10 = bf16[128,1280]{1,0:T(8,128)(2,1)} collective-permute-done((bf16[128,1280]{1,0:T(8,128)(2,1)S(1)}, bf16[128,1280]{1,0:T(8,128)(2,1)}, u32[]{:S(2)}, u32[]{:S(2)}) %collective-permute-start.10) | collective-permute-done | bytes 327712 | tf_op jit(solution)/shard_map/ppermute | solution.py:65
  155.0 5.3 %multiply_convert_fusion = bf16[8,144,1536]{2,1,0:T(8,128)(2,1)} fusion(f32[8,144]{1,0:T(8,128)S(1)} %select_reduce_fusion, bf16[128,1536]{1,0:T(8,128)(2,1)} %copy-done.39, bf16[128,1536]{1,0:T(8,128)(2,1)} %copy-done.40, bf16[128,1536]{1,0:T(8,128)(2,1)} %copy-done.41, bf16[128,1536]{1,0:T(8,128)(2,1)} %copy-done.25, s32[8,512]{1,0:T(8,128)S(1)} %fusion.114), kind=kOutput, calls=%fused_computation.9 | convolution fusion | flops 1822359552 | bytes 5132800 | tf_op jit(solution)/shard_map/dot_general | solution.py:13
  168.0 20.8 %all-to-all-done.2 = bf16[8,144,1280]{2,1,0:T(8,128)(2,1)S(1)} async-done(((bf16[8,144,1280]{2,1,0:T(8,128)(2,1)}), bf16[8,144,1280]{2,1,0:T(8,128)(2,1)S(1)}, u32[]{:S(2)}, u32[]{:S(2)}) %all-to-all-start.2) | async-done | bytes 2949152 | tf_op jit(solution)/shard_map/all_to_all | solution.py:68
  193.4 5.8 %fusion.36 = f32[1152,768]{1,0:T(8,128)} fusion(bf16[1152,1280]{1,0:T(8,128)(2,1)S(1)} %bitcast.344, bf16[768,4096]{1,0:T(8,128)(2,1)} %bitcast.372), kind=kOutput, calls=%fused_computation.75 | convolution fusion | flops 2264924160 | bytes 8454144 | tf_op jit(solution)/shard_map/dot_general | solution.py:13
  214.8 20.7 %collective-permute-done.35 = bf16[144,32]{0,1:T(8,128)(2,1)S(1)} collective-permute-done((bf16[144,32]{0,1:T(8,128)(2,1)S(1)}, bf16[144,32]{0,1:T(8,128)(2,1)S(1)}, u32[]{:S(2)}, u32[]{:S(2)}) %collective-permute-start.35) | collective-permute-done | bytes 9248 | tf_op jit(solution)/shard_map/ppermute | solution.py:24
  242.2 5.8 %fusion.27 = f32[1152,768]{1,0:T(8,128)S(1)} fusion(bf16[1152,1536]{1,0:T(8,128)(2,1)} %bitcast.18, bf16[768,4096]{1,0:T(8,128)(2,1)} %bitcast.373), kind=kOutput, calls=%fused_computation.55 | convolution fusion | flops 2717908992 | bytes 9437184 | tf_op jit(solution)/shard_map/dot_general | solution.py:13
  264.4 5.0 fusion.39
  294.6 26.6 %collective-permute-done.28 = bf16[144,32]{0,1:T(8,128)(2,1)S(1)} collective-permute-done((bf16[144,32]{0,1:T(8,128)(2,1)S(1)}, bf16[144,32]{0,1:T(8,128)(2,1)S(1)}, u32[]{:S(2)}, u32[]{:S(2)}) %collective-permute-start.28) | collective-permute-done | bytes 9248 | tf_op jit(solution)/shard_map/ppermute | solution.py:24
  328.2 5.5 %convolution_multiply_fusion = f32[256,4096]{1,0:T(8,128)} fusion(bf16[256,512]{0,1:T(8,128)(2,1)S(1)} %bitcast.361, bf16[512,4096]{1,0:T(8,128)(2,1)} %all-gather.3.cloned.1.call-done), kind=kOutput, calls=%fused_computation.11 | convolution fusion | flops 1074790400 | bytes 8650752 | tf_op jit(solution)/shard_map/dot_general | solution.py:13
  336.9 6.3 %fusion.53 = f32[1152,1024]{1,0:T(8,128)} fusion(bf16[1152,768]{1,0:T(8,128)(2,1)} %copy-done.16, bf16[1,4096,768]{2,1,0:T(8,128)(2,1)} %param.20), kind=kOutput, calls=%fused_computation.91 | convolution fusion | flops 1811939328 | bytes 8060928 | tf_op jit(solution)/shard_map/dot_general | solution.py:13
  343.2 4.8 convolution_add_fusion.6
  367.4 22.8 %collective-permute-start.15 = (bf16[128,1024]{1,0:T(8,128)(2,1)}, bf16[128,1024]{1,0:T(8,128)(2,1)S(1)}, u32[]{:S(2)}, u32[]{:S(2)}) collective-permute-start(bf16[128,1024]{1,0:T(8,128)(2,1)} %fusion.72), channel_id=1, source_target_pairs={{3,0},{0,1},{1,2},{2,3},{7,4},{4,5},{5,6},{6,7},{11,8},{8,9},{9,10... | collective-permute-start | bytes 786440 | tf_op jit(solution)/shard_map/ppermute | solution.py:65
  391.5 7.2 %all-to-all-done.5 = bf16[8,144,1280]{2,1,0:T(8,128)(2,1)S(1)} async-done(((bf16[8,144,1280]{2,1,0:T(8,128)(2,1)}), bf16[8,144,1280]{2,1,0:T(8,128)(2,1)S(1)}, u32[]{:S(2)}, u32[]{:S(2)}) %all-to-all-start.5) | async-done | bytes 2949152 | tf_op jit(solution)/shard_map/all_to_all | solution.py:68
  405.5 16.5 %collective-permute-start.17 = (bf16[128,1024]{1,0:T(8,128)(2,1)S(1)}, bf16[128,1024]{1,0:T(8,128)(2,1)S(1)}, u32[]{:S(2)}, u32[]{:S(2)}) collective-permute-start(bf16[128,1024]{1,0:T(8,128)(2,1)S(1)} %fusion.74), channel_id=1, source_target_pairs={{1,0},{2,1},{3,2},{0,3},{5,4},{6,5},{7,6},{4,7},{9,8},{10,9},{11,1... | collective-permute-start | bytes 786440 | tf_op jit(solution)/shard_map/ppermute | solution.py:65
  422.6 8.6 %collective-permute-start.18 = (bf16[128,1280]{1,0:T(8,128)(2,1)S(1)}, bf16[128,1280]{1,0:T(8,128)(2,1)S(1)}, u32[]{:S(2)}, u32[]{:S(2)}) collective-permute-start(bf16[128,1280]{1,0:T(8,128)(2,1)S(1)} %fusion.24), channel_id=1, source_target_pairs={{3,0},{0,1},{1,2},{2,3},{7,4},{4,5},{5,6},{6,7},{11,8},{8,9},{9,10... | collective-permute-start | bytes 983048 | tf_op jit(solution)/shard_map/ppermute | solution.py:65
  438.1 6.3 %collective-permute-done.17 = bf16[128,1024]{1,0:T(8,128)(2,1)S(1)} collective-permute-done((bf16[128,1024]{1,0:T(8,128)(2,1)S(1)}, bf16[128,1024]{1,0:T(8,128)(2,1)S(1)}, u32[]{:S(2)}, u32[]{:S(2)}) %collective-permute-start.17) | collective-permute-done | bytes 262176 | tf_op jit(solution)/shard_map/ppermute | solution.py:65
  446.7 13.2 %collective-permute-done.19 = bf16[128,1280]{1,0:T(8,128)(2,1)S(1)} collective-permute-done((bf16[128,1280]{1,0:T(8,128)(2,1)S(1)}, bf16[128,1280]{1,0:T(8,128)(2,1)S(1)}, u32[]{:S(2)}, u32[]{:S(2)}) %collective-permute-start.19) | collective-permute-done | bytes 327712 | tf_op jit(solution)/shard_map/ppermute | solution.py:65
  469.5 6.8 %collective-permute-start.21 = (bf16[128,1024]{1,0:T(8,128)(2,1)}, bf16[128,1024]{1,0:T(8,128)(2,1)S(1)}, u32[]{:S(2)}, u32[]{:S(2)}) collective-permute-start(bf16[128,1024]{1,0:T(8,128)(2,1)} %fusion.75), channel_id=1, source_target_pairs={{3,0},{0,1},{1,2},{2,3},{7,4},{4,5},{5,6},{6,7},{11,8},{8,9},{9,10... | collective-permute-start | bytes 786440 | tf_op jit(solution)/shard_map/ppermute | solution.py:65
  489.5 6.9 %collective-permute-start.24 = (bf16[128,768]{1,0:T(8,128)(2,1)S(1)}, bf16[128,768]{1,0:T(8,128)(2,1)S(1)}, u32[]{:S(2)}, u32[]{:S(2)}) collective-permute-start(bf16[128,768]{1,0:T(8,128)(2,1)S(1)} %fusion.92), channel_id=1, source_target_pairs={{3,0},{0,1},{1,2},{2,3},{7,4},{4,5},{5,6},{6,7},{11,8},{8,9},{9,10... | collective-permute-start | bytes 589832 | tf_op jit(solution)/shard_map/ppermute | solution.py:65
  503.9 8.7 %collective-permute-done.25 = bf16[128,768]{1,0:T(8,128)(2,1)S(1)} collective-permute-done((bf16[128,768]{1,0:T(8,128)(2,1)S(1)}, bf16[128,768]{1,0:T(8,128)(2,1)S(1)}, u32[]{:S(2)}, u32[]{:S(2)}) %collective-permute-start.25) | collective-permute-done | bytes 196640 | tf_op jit(solution)/shard_map/ppermute | solution.py:65
  (303 shorter events, 221.6 us)
Async XLA Ops:
  7.2 193.5 %all-gather.5.cloned.1.call-start = ((), (), s32[]{:S(2)}) async-start(), calls=%async_computation.11 | async-start | bytes 2359296 | tf_op jit(solution)/shard_map/all_gather | solution.py:107
  14.2 28.1 %collective-permute-start.13 = (bf16[128,1536]{1,0:T(8,128)(2,1)S(1)}, bf16[128,1536]{1,0:T(8,128)(2,1)S(1)}, u32[]{:S(2)}, u32[]{:S(2)}) collective-permute-start(bf16[128,1536]{1,0:T(8,128)(2,1)S(1)} %slice.194), channel_id=1, source_target_pairs={{2,0},{3,1},{0,2},{1,3},{6,4},{7,5},{4,6},{5,7},{10,8},{11,9},{8,1... | collective-permute-start | bytes 1179656 | tf_op jit(solution)/shard_map/ppermute | solution.py:65
  42.4 158.3 %all-gather.3.cloned.1.call-start = ((), (), s32[]{:S(2)}) async-start(), calls=%async_computation.9 | async-start | bytes 5242880 | tf_op jit(solution)/shard_map/all_gather | solution.py:106
  77.6 65.5 %collective-permute-start.10 = (bf16[128,1280]{1,0:T(8,128)(2,1)S(1)}, bf16[128,1280]{1,0:T(8,128)(2,1)}, u32[]{:S(2)}, u32[]{:S(2)}) collective-permute-start(bf16[128,1280]{1,0:T(8,128)(2,1)S(1)} %slice.192), channel_id=1, source_target_pairs={{2,0},{3,1},{0,2},{1,3},{6,4},{7,5},{4,6},{5,7},{10,8},{11,9},{8,1... | collective-permute-start | bytes 983048 | tf_op jit(solution)/shard_map/ppermute | solution.py:65
  81.6 61.6 %collective-permute-start.9 = (bf16[128,1280]{1,0:T(8,128)(2,1)S(1)}, bf16[128,1280]{1,0:T(8,128)(2,1)}, u32[]{:S(2)}, u32[]{:S(2)}) collective-permute-start(bf16[128,1280]{1,0:T(8,128)(2,1)S(1)} %slice.192), channel_id=1, source_target_pairs={{1,0},{2,1},{3,2},{0,3},{5,4},{6,5},{7,6},{4,7},{9,8},{10,9},{11,1... | collective-permute-start | bytes 983048 | tf_op jit(solution)/shard_map/ppermute | solution.py:65
  92.5 55.2 %all-to-all-start.1 = ((bf16[8,144,768]{2,1,0:T(8,128)(2,1)}), bf16[8,144,768]{2,1,0:T(8,128)(2,1)S(1)}, u32[]{:S(2)}, u32[]{:S(2)}) async-start(bf16[8,144,768]{2,1,0:T(8,128)(2,1)} %multiply_convert_fusion.3), calls=%async_computation.1 | async-start | bytes 3538944 | tf_op jit(solution)/shard_map/all_to_all | solution.py:68
  149.1 39.8 %all-to-all-start.2 = ((bf16[8,144,1280]{2,1,0:T(8,128)(2,1)}), bf16[8,144,1280]{2,1,0:T(8,128)(2,1)S(1)}, u32[]{:S(2)}, u32[]{:S(2)}) async-start(bf16[8,144,1280]{2,1,0:T(8,128)(2,1)} %multiply_convert_fusion.1), calls=%async_computation.2 | async-start | bytes 5898240 | tf_op jit(solution)/shard_map/all_to_all | solution.py:68
  188.8 50.8 %all-to-all-start.3 = ((bf16[8,144,1536]{2,1,0:T(8,128)(2,1)}), bf16[8,144,1536]{2,1,0:T(8,128)(2,1)}, u32[]{:S(2)}, u32[]{:S(2)}) async-start(bf16[8,144,1536]{2,1,0:T(8,128)(2,1)} %multiply_convert_fusion), calls=%async_computation.3 | async-start | bytes 7077888 | tf_op jit(solution)/shard_map/all_to_all | solution.py:68
  208.6 30.2 %collective-permute-start.40 = (bf16[144,32]{0,1:T(8,128)(2,1)S(1)}, bf16[144,32]{0,1:T(8,128)(2,1)S(1)}, u32[]{:S(2)}, u32[]{:S(2)}) collective-permute-start(bf16[144,32]{0,1:T(8,128)(2,1)S(1)} %get-tuple-element.39), channel_id=1, source_target_pairs={{0,28},{4,24},{8,20},{12,16},{16,12},{20,8},{24,4},{28,0},{1,29},{... | collective-permute-start | bytes 27656 | tf_op jit(solution)/shard_map/ppermute | solution.py:24
  211.2 27.6 %collective-permute-start.39 = (bf16[144,32]{0,1:T(8,128)(2,1)S(1)}, bf16[144,32]{0,1:T(8,128)(2,1)S(1)}, u32[]{:S(2)}, u32[]{:S(2)}) collective-permute-start(bf16[144,32]{0,1:T(8,128)(2,1)S(1)} %get-tuple-element.40), channel_id=1, source_target_pairs={{0,24},{4,28},{8,16},{12,20},{16,8},{20,12},{24,0},{28,4},{1,25},{... | collective-permute-start | bytes 27656 | tf_op jit(solution)/shard_map/ppermute | solution.py:24
  271.4 53.0 %collective-permute-start.33 = (bf16[144,32]{0,1:T(8,128)(2,1)S(1)}, bf16[144,32]{0,1:T(8,128)(2,1)S(1)}, u32[]{:S(2)}, u32[]{:S(2)}) collective-permute-start(bf16[144,32]{0,1:T(8,128)(2,1)S(1)} %get-tuple-element.47), channel_id=1, source_target_pairs={{0,28},{4,24},{8,20},{12,16},{16,12},{20,8},{24,4},{28,0},{1,29},{... | collective-permute-start | bytes 27656 | tf_op jit(solution)/shard_map/ppermute | solution.py:24
  272.8 51.6 %collective-permute-start.32 = (bf16[144,32]{0,1:T(8,128)(2,1)S(1)}, bf16[144,32]{0,1:T(8,128)(2,1)S(1)}, u32[]{:S(2)}, u32[]{:S(2)}) collective-permute-start(bf16[144,32]{0,1:T(8,128)(2,1)S(1)} %get-tuple-element.48), channel_id=1, source_target_pairs={{0,24},{4,28},{8,16},{12,20},{16,8},{20,12},{24,0},{28,4},{1,25},{... | collective-permute-start | bytes 27656 | tf_op jit(solution)/shard_map/ppermute | solution.py:24
  274.1 50.3 %collective-permute-start.31 = (bf16[144,32]{0,1:T(8,128)(2,1)S(1)}, bf16[144,32]{0,1:T(8,128)(2,1)S(1)}, u32[]{:S(2)}, u32[]{:S(2)}) collective-permute-start(bf16[144,32]{0,1:T(8,128)(2,1)S(1)} %get-tuple-element.49), channel_id=1, source_target_pairs={{0,20},{4,16},{8,28},{12,24},{16,4},{20,0},{24,12},{28,8},{1,21},{... | collective-permute-start | bytes 27656 | tf_op jit(solution)/shard_map/ppermute | solution.py:24
  275.3 49.1 %collective-permute-start.30 = (bf16[144,32]{0,1:T(8,128)(2,1)S(1)}, bf16[144,32]{0,1:T(8,128)(2,1)S(1)}, u32[]{:S(2)}, u32[]{:S(2)}) collective-permute-start(bf16[144,32]{0,1:T(8,128)(2,1)S(1)} %get-tuple-element.50), channel_id=1, source_target_pairs={{0,16},{4,20},{8,24},{12,28},{16,0},{20,4},{24,8},{28,12},{1,17},{... | collective-permute-start | bytes 27656 | tf_op jit(solution)/shard_map/ppermute | solution.py:24
  288.6 59.4 %all-to-all-start.4 = ((bf16[8,144,1024]{2,1,0:T(8,128)(2,1)}), bf16[8,144,1024]{2,1,0:T(8,128)(2,1)S(1)}, u32[]{:S(2)}, u32[]{:S(2)}) async-start(bf16[8,144,1024]{2,1,0:T(8,128)(2,1)} %bitcast.354), calls=%async_computation.4 | async-start | bytes 4718592 | tf_op jit(solution)/shard_map/all_to_all | solution.py:68
  292.4 168.2 %reduce-scatter.2.cloned.1.call-start = ((), (), s32[]{:S(2)}) async-start(), calls=%async_computation.10 | async-start | bytes 4718592 | tf_op jit(solution)/shard_map/reduce_scatter | solution.py:158
  292.6 28.6 %collective-permute-start.28 = (bf16[144,32]{0,1:T(8,128)(2,1)S(1)}, bf16[144,32]{0,1:T(8,128)(2,1)S(1)}, u32[]{:S(2)}, u32[]{:S(2)}) collective-permute-start(bf16[144,32]{0,1:T(8,128)(2,1)S(1)} %get-tuple-element.52), channel_id=1, source_target_pairs={{0,8},{4,12},{8,0},{12,4},{16,24},{20,28},{24,16},{28,20},{1,9},{5... | collective-permute-start | bytes 27656 | tf_op jit(solution)/shard_map/ppermute | solution.py:24
  349.4 49.2 %all-to-all-start.5 = ((bf16[8,144,1280]{2,1,0:T(8,128)(2,1)}), bf16[8,144,1280]{2,1,0:T(8,128)(2,1)S(1)}, u32[]{:S(2)}, u32[]{:S(2)}) async-start(bf16[8,144,1280]{2,1,0:T(8,128)(2,1)} %bitcast.353), calls=%async_computation.5 | async-start | bytes 5898240 | tf_op jit(solution)/shard_map/all_to_all | solution.py:68
  367.4 66.8 %collective-permute-start.15 = (bf16[128,1024]{1,0:T(8,128)(2,1)}, bf16[128,1024]{1,0:T(8,128)(2,1)S(1)}, u32[]{:S(2)}, u32[]{:S(2)}) collective-permute-start(bf16[128,1024]{1,0:T(8,128)(2,1)} %fusion.72), channel_id=1, source_target_pairs={{3,0},{0,1},{1,2},{2,3},{7,4},{4,5},{5,6},{6,7},{11,8},{8,9},{9,10... | collective-permute-start | bytes 786440 | tf_op jit(solution)/shard_map/ppermute | solution.py:65
  391.5 46.6 %collective-permute-start.16 = (bf16[128,1024]{1,0:T(8,128)(2,1)}, bf16[128,1024]{1,0:T(8,128)(2,1)}, u32[]{:S(2)}, u32[]{:S(2)}) collective-permute-start(bf16[128,1024]{1,0:T(8,128)(2,1)} %fusion.73), channel_id=1, source_target_pairs={{2,0},{3,1},{0,2},{1,3},{6,4},{7,5},{4,6},{5,7},{10,8},{11,9},{8,1... | collective-permute-start | bytes 786440 | tf_op jit(solution)/shard_map/ppermute | solution.py:65
  398.7 63.1 %all-to-all-start.6 = ((bf16[8,144,1024]{2,1,0:T(8,128)(2,1)}), bf16[8,144,1024]{2,1,0:T(8,128)(2,1)}, u32[]{:S(2)}, u32[]{:S(2)}) async-start(bf16[8,144,1024]{2,1,0:T(8,128)(2,1)} %bitcast.355), calls=%async_computation.6 | async-start | bytes 4718592 | tf_op jit(solution)/shard_map/all_to_all | solution.py:68
  405.5 38.9 %collective-permute-start.17 = (bf16[128,1024]{1,0:T(8,128)(2,1)S(1)}, bf16[128,1024]{1,0:T(8,128)(2,1)S(1)}, u32[]{:S(2)}, u32[]{:S(2)}) collective-permute-start(bf16[128,1024]{1,0:T(8,128)(2,1)S(1)} %fusion.74), channel_id=1, source_target_pairs={{1,0},{2,1},{3,2},{0,3},{5,4},{6,5},{7,6},{4,7},{9,8},{10,9},{11,1... | collective-permute-start | bytes 786440 | tf_op jit(solution)/shard_map/ppermute | solution.py:65
  431.9 28.0 %collective-permute-start.19 = (bf16[128,1280]{1,0:T(8,128)(2,1)S(1)}, bf16[128,1280]{1,0:T(8,128)(2,1)S(1)}, u32[]{:S(2)}, u32[]{:S(2)}) collective-permute-start(bf16[128,1280]{1,0:T(8,128)(2,1)S(1)} %fusion.25), channel_id=1, source_target_pairs={{2,0},{3,1},{0,2},{1,3},{6,4},{7,5},{4,6},{5,7},{10,8},{11,9},{8,1... | collective-permute-start | bytes 983048 | tf_op jit(solution)/shard_map/ppermute | solution.py:65
  469.5 28.0 %collective-permute-start.21 = (bf16[128,1024]{1,0:T(8,128)(2,1)}, bf16[128,1024]{1,0:T(8,128)(2,1)S(1)}, u32[]{:S(2)}, u32[]{:S(2)}) collective-permute-start(bf16[128,1024]{1,0:T(8,128)(2,1)} %fusion.75), channel_id=1, source_target_pairs={{3,0},{0,1},{1,2},{2,3},{7,4},{4,5},{5,6},{6,7},{11,8},{8,9},{9,10... | collective-permute-start | bytes 786440 | tf_op jit(solution)/shard_map/ppermute | solution.py:65
  (79 other events, 1124.5 us)
Sparse Core Ops, SparseCore 0:
  42.5 36.7 all-gather.4
  80.8 108.9 all-gather.2
  333.9 101.9 reduce-scatter.1
